TPU v7x, 32 devices: a whole 2x2x4 slice. The times are simulated.
32 devices in a mesh: groups: 2 (over x), space: 8 (over z, y), rep: 2 (over core).
Axes of the slice: x: 2, y: 2, z: 4, core: 2. Of those that a mesh axis runs over, the one named last changes fastest.
Arguments:
- features: bfloat16 [2, 64, 8, 8, 512], P('rep', ('groups', 'space')), parts along dimension 1, may hold values from -6 to 6
- weight_one: bfloat16 [27, 64, 64], replicated, may hold values from -0.15625 to 0.15625
- weight_two: bfloat16 [27, 64, 64], replicated, may hold values from -0.15625 to 0.15625
- grad_out: bfloat16 [2, 64, 8, 8, 512], P('rep', ('groups', 'space')), parts along dimension 1, may hold values from -0.125 to 0.125
- active: int32 [2, 64, 512], P('rep', ('groups', 'space')), parts along dimension 1, may hold values 0 or 1
- send_list: int32 [2, 16, 8, 2], P('rep', ('groups', 'space')), parts along dimension 1, may hold values from 0 to 4, as said below
- local_nbr: int32 [2, 64, 27], P('rep', ('groups', 'space')), parts along dimension 1, may hold values from 0 to 20, as said below
Outputs:
- output: bfloat16 [2, 64, 8, 8, 512], P('rep', ('groups', 'space')), parts along dimension 1
- grad_one: float32 [54, 64, 64], P('groups'), parts along dimension 0
- grad_two: float32 [54, 64, 64], P('groups'), parts along dimension 0
There are 2 independent parts, one for each index of `groups`. A program takes and returns all parts, laid end to end along the dimension named above; an argument that names none is the same for every part. Nothing has to cross between parts.
Inputs may be any that keep to these rules, and one draw needn't show every extreme that they name: Owners form two rows of 4: owner o is in row o // 4 at column o % 4. send_list[r, o, k, :] lists distinct local indices (below 4) of o's bricks that owner o + delta[k] reads, then the padding 4. Real bricks go only to an owner of the same row at column distance one, or of the other row at column distance at most one, so every entry is 4 where o + delta[k] is no such owner; the two owners of a column send each other exactly 2 bricks. local_nbr[r, n, d] indexes the table of the owner o of brick n: below 4 one of o's bricks, 4 + k * 2 + s the brick of send_list[r, o - delta[k], k, s], and 20 the empty brick. Entries of the middle kind name only slots that hold a real brick; direction 13 names the brick itself.
All inputs are finite; a program needn't handle non-finite values. No bound on the sum of `active` on one device may be relied on, other than what follows from the above.
Results may differ from a plain program's by a relative error of at most 0.005.
Values may be sent and summed in bfloat16 or wider, within the bound.
A program may use at most 128 MiB of HBM per device.

v0:
```python
import functools

import jax
import jax.numpy as jnp
from jax import lax
from jax.experimental import pallas as pl
from jax.experimental.pallas import tpu as pltpu
from jax.sharding import PartitionSpec as P

BE = 8
F32 = jnp.float32
BF16 = jnp.bfloat16
LIMIT = 48 * 1024 * 1024
VM = pl.BlockSpec(memory_space=pltpu.VMEM)
SM = pl.BlockSpec(memory_space=pltpu.SMEM)


def from_behind(value, axis, steps):
    count = lax.axis_size(axis)
    initial, last = (max(0, -steps), min(count, count - steps))
    return lax.ppermute(value, axis, [(source, source + steps) for source in range(initial, last)])


def iota(shape, dim):
    return lax.broadcasted_iota(jnp.int32, shape, dim)


def expand_mask(mask_ref):
    rows, edge = mask_ref.shape
    width = edge * 64
    spread = (iota((edge, width), 1) // 64 == iota((edge, width), 0)).astype(BF16)
    wide = jnp.dot(mask_ref[...].astype(BF16), spread, preferred_element_type=F32)
    return wide.reshape(BE, rows // BE, width)


def to_rows(ref):
    return jnp.concatenate([ref[b].astype(F32) for b in range(ref.shape[0])], axis=1)


def fill_outbound(send_ref, bricks_ref, out_refs):
    last = bricks_ref.shape[0] - 1
    for k, out in enumerate(out_refs):
        for s in range(out.shape[0]):
            out[s] = bricks_ref[jnp.minimum(send_ref[k, s], last)]


def fill_table(table_ref, own_ref, received):
    bricks = own_ref.shape[0]
    table_ref[0:bricks] = own_ref[...]
    row = bricks
    for ref in received:
        count = ref.shape[0]
        table_ref[row : row + count] = ref[...]
        row += count
    table_ref[row] = jnp.zeros(table_ref.shape[1:], table_ref.dtype)


def assemble(table_ref, nbr_ref, shifted_ref):
    width = table_ref.shape[3]
    lanes = iota((BE, 128), 1)
    rows = iota((BE, width + 128), 0)

    def plane(b, direction, source):
        strips = []
        for j in range(3):
            first = direction + 3 * j
            mid = table_ref[nbr_ref[b, first + 1], source].astype(F32)
            low = table_ref[nbr_ref[b, first], source, :, width - 128 : width].astype(F32)
            high = table_ref[nbr_ref[b, first + 2], source, :, 0:128].astype(F32)
            end = mid[:, width - 128 :]
            body = jnp.concatenate(
                [mid[:, : width - 128], jnp.where(lanes >= 64, low, end)], axis=1
            )
            tail = jnp.where(lanes < 64, high, end)
            strips.append(
                jnp.concatenate([pltpu.roll(body, 64, 1), pltpu.roll(tail, 64, 1)], axis=1)
            )
        before = pltpu.roll(jnp.where(rows == BE - 1, strips[0], strips[1]), 1, 0)
        after = pltpu.roll(jnp.where(rows == 0, strips[2], strips[1]), BE - 1, 0)
        return before, strips[1], after

    def step(x, carry):
        side = jnp.where(x == 0, 0, jnp.where(x == BE + 1, 2, 1))
        source = lax.rem(x + BE - 1, BE)
        for pair in range(nbr_ref.shape[0] // 2):
            one = plane(2 * pair, 9 * side, source)
            two = plane(2 * pair + 1, 9 * side, source)
            for j in range(3):
                both = jnp.concatenate([one[j], two[j]], axis=0).astype(BF16)
                shifted_ref[j, x, 16 * pair : 16 * pair + 16, :] = both
        return carry

    lax.fori_loop(0, BE + 2, step, 0)


def banded_conv(shifted_ref, kernel_ref, result_ref):
    length, rows, width = result_ref.shape

    def step(p, carry):
        at = pl.multiple_of(p * 128, 128)
        total = jnp.zeros((length * rows, 128), F32)
        for i in range(3):
            for j in range(3):
                block = shifted_ref[j, i : i + length, :, pl.ds(at, 256)]
                total = total + jnp.dot(
                    block.reshape(length * rows, 256),
                    kernel_ref[3 * i + j],
                    preferred_element_type=F32,
                )
        result_ref[:, :, pl.ds(at, 128)] = total.reshape(length, rows, 128)
        return carry

    lax.fori_loop(0, width // 128, step, 0)


def banded_grad(shifted_ref, upward, grad_ref):
    rows, width = upward.shape
    turned = [
        upward[:, 128 * p : 128 * p + 128].T.astype(BF16) for p in range(width // 128)
    ]

    def step(i, carry):
        for j in range(3):
            total = jnp.zeros((128, 256), F32)
            for p in range(width // 128):
                block = shifted_ref[j, pl.ds(i, BE), :, 128 * p : 128 * p + 256]
                total = total + jnp.dot(
                    turned[p], block.reshape(rows, 256), preferred_element_type=F32
                )
            flat = total.T
            for k in range(3):
                grad_ref[9 * i + 3 * j + k] = (
                    flat[64 * k : 64 * k + 64, 0:64] + flat[64 * k + 64 : 64 * k + 128, 64:128]
                )
        return carry

    lax.fori_loop(0, 3, step, 0)


def mask_kernel(send_ref, features_ref, mask_ref, x_ref, *out_refs):
    wide = expand_mask(mask_ref)
    for b in range(x_ref.shape[0]):
        part = wide[:, BE * b : BE * b + BE, :]
        x_ref[b] = (features_ref[b].astype(F32) * part).astype(BF16)
    fill_outbound(send_ref, x_ref, out_refs)


def spread_kernel(nbr_ref, up_ref, mask_ref, kernel_ref, own_ref, *rest):
    out_refs, (shifted_ref, spread_ref, totals_ref) = rest[:-3], rest[-3:]
    bricks, width = own_ref.shape[0], own_ref.shape[3]
    wide = expand_mask(mask_ref)
    up = (to_rows(up_ref) * wide).astype(BF16).astype(F32)
    for j in range(3):
        for x in (0, 1, BE + 2, BE + 3):
            shifted_ref[j, x] = jnp.zeros(shifted_ref.shape[2:], BF16)
    for x in range(BE):
        for b in range(bricks):
            tile = up[x, BE * b : BE * b + BE, :]
            side = jnp.zeros((BE, 128), F32)
            tile = jnp.concatenate([side, tile, side], axis=1)
            tile = jnp.concatenate([tile, jnp.zeros_like(tile)], axis=0)
            for j in range(3):
                moved = pltpu.roll(tile, 2 - j, 0) if j < 2 else tile
                shifted_ref[j, x + 2, 16 * b : 16 * b + 16, :] = moved.astype(BF16)
    banded_conv(shifted_ref, kernel_ref, spread_ref)

    def clear(t, carry):
        totals_ref[t] = jnp.zeros(totals_ref.shape[1:], F32)
        return carry

    lax.fori_loop(0, totals_ref.shape[0], clear, 0)
    lanes = iota((BE, 128), 1)
    rows = iota((BE, width), 0)
    rows_short = iota((BE, 128), 0)

    def deposit(x, carry):
        side = jnp.where(x == 0, 0, jnp.where(x == BE + 1, 2, 1))
        target = lax.rem(x + BE - 1, BE)
        for b in range(bricks):
            tile = spread_ref[x, 16 * b : 16 * b + 16, :]
            tile = pltpu.roll(pltpu.roll(tile, width + 64, 1), 15, 0)
            for j in range(3):
                first = 9 * side + 3 * j
                body = tile[0:BE, 0:width] if j == 1 else tile[BE : 2 * BE, 0:width]
                ends = tile[0:BE, width:] if j == 1 else tile[BE : 2 * BE, width:]
                if j != 1:
                    keep = BE - 1 if j == 0 else 0
                    body = jnp.where(rows == keep, body, 0.0)
                    ends = jnp.where(rows_short == keep, ends, 0.0)
                totals_ref[nbr_ref[b, first + 1], target] += body
                totals_ref[nbr_ref[b, first], target, :, width - 128 : width] += jnp.where(
                    lanes >= 64, ends, 0.0
                )
                totals_ref[nbr_ref[b, first + 2], target, :, 0:128] += jnp.where(
                    lanes < 64, ends, 0.0
                )
        return carry

    lax.fori_loop(0, BE + 2, deposit, 0)
    own_ref[...] = totals_ref[0:bricks]
    row = bricks
    for out in out_refs:
        count = out.shape[0]
        out[...] = totals_ref[row : row + count].astype(BF16)
        row += count


def first_kernel(count, send_ref, nbr_ref, x_ref, mask_ref, kernel_ref, *rest):
    received, rest = rest[:count], rest[count:]
    pre_ref, shifted_ref, hidden_ref = rest[:3]
    out_refs, (table_ref,) = rest[3:-1], rest[-1:]
    fill_table(table_ref, x_ref, received)
    assemble(table_ref, nbr_ref, shifted_ref)
    banded_conv(shifted_ref, kernel_ref, pre_ref)
    pre = pre_ref[...]
    hidden = expand_mask(mask_ref) * (pre * jax.nn.sigmoid(pre))
    for b in range(hidden_ref.shape[0]):
        hidden_ref[b] = hidden[:, BE * b : BE * b + BE, :].astype(BF16)
    fill_outbound(send_ref, hidden_ref, out_refs)


def inner_kernel(send_ref, mask_ref, pre_ref, shifted_ref, own_ref, *rest):
    received, (grad_ref, home_ref) = rest[:-2], rest[-2:]
    bricks = own_ref.shape[0]
    home_ref[0:bricks] = own_ref[...]
    for k, ref in enumerate(received):
        for s in range(ref.shape[0]):
            home_ref[send_ref[k, s]] += ref[s].astype(F32)
    back = jnp.concatenate([home_ref[b] for b in range(bricks)], axis=1)
    pre = pre_ref[...]
    logistic = jax.nn.sigmoid(pre)
    slope = logistic * (1.0 + pre * (1.0 - logistic))
    inner = (expand_mask(mask_ref) * back * slope).astype(BF16).astype(F32)
    banded_grad(shifted_ref, inner.reshape(-1, inner.shape[2]), grad_ref)


def second_kernel(nbr_ref, hidden_ref, up_ref, mask_ref, kernel_ref, *rest):
    received, (output_ref, grad_ref, table_ref, shifted_ref, post_ref) = rest[:-5], rest[-5:]
    fill_table(table_ref, hidden_ref, received)
    assemble(table_ref, nbr_ref, shifted_ref)
    wide = expand_mask(mask_ref)
    up = (to_rows(up_ref) * wide).astype(BF16).astype(F32)
    banded_grad(shifted_ref, up.reshape(-1, up.shape[2]), grad_ref)
    banded_conv(shifted_ref, kernel_ref, post_ref)
    post = post_ref[...] * wide
    for b in range(output_ref.shape[0]):
        output_ref[b] = post[:, BE * b : BE * b + BE, :].astype(BF16)


def banded(weight):
    split = weight.reshape(9, 3, 64, 64)
    left = jnp.pad(split, ((0, 0), (0, 1), (0, 0), (0, 0)))
    right = jnp.pad(split, ((0, 0), (1, 0), (0, 0), (0, 0)))
    return jnp.concatenate([left, right], axis=-1).reshape(9, 256, 128)


def call(body, specs, outs, scratch, args):
    return pl.pallas_call(
        body,
        out_shape=outs,
        in_specs=specs,
        out_specs=[VM] * len(outs),
        scratch_shapes=scratch,
        compiler_params=pltpu.CompilerParams(vmem_limit_bytes=LIMIT),
    )(*args)


def per_device(features, weight_one, weight_two, grad_out, active, send_list, local_nbr):
    bricks = features.shape[1]
    width = features.shape[4]
    brick = features.shape[2:]
    send = send_list[0, 0]
    nbr = local_nbr[0]
    owners = lax.axis_size("space")
    slots = send.shape[1]
    half = owners // 2
    deltas = [-1, 1, half - 1, half, half + 1, -half - 1, -half, 1 - half]
    mask = active[0].reshape(bricks, BE, BE, BE).transpose(1, 0, 2, 3).reshape(-1, BE)
    mask = mask.astype(F32)
    kernel_one = banded(weight_one)
    kernel_two = banded(weight_two)
    kernel_back = banded(jnp.flip(weight_two, 0).transpose(0, 2, 1))

    shape = jax.ShapeDtypeStruct
    outbound = [shape((slots,) + brick, BF16)] * len(deltas)
    bricks_half = shape((bricks,) + brick, BF16)
    bricks_full = shape((bricks,) + brick, F32)
    entries = bricks + len(deltas) * slots + 1
    rows = bricks * BE
    table = pltpu.VMEM((entries,) + brick, BF16)
    shifted = (3, BE + 2, rows, width + 128)
    grads = shape(weight_one.shape, F32)
    pre_shape = (BE, rows, width)

    x, *sends = call(
        mask_kernel, [SM, VM, VM], [bricks_half] + outbound, [], (send, features[0], mask)
    )
    x_in = [from_behind(v, "space", d) for v, d in zip(sends, deltas)]
    own_back, *sends = call(
        spread_kernel,
        [SM, VM, VM, VM],
        [bricks_full] + outbound,
        [
            pltpu.VMEM((3, BE + 4, 16 * bricks, width + 256), BF16),
            pltpu.VMEM((BE + 2, 16 * bricks, width + 128), F32),
            pltpu.VMEM((entries,) + brick, F32),
        ],
        (nbr, grad_out[0], mask, kernel_back),
    )
    back_in = [from_behind(v, "space", -d) for v, d in zip(sends, deltas)]
    pre, windows, hidden, *sends = call(
        functools.partial(first_kernel, len(deltas)),
        [SM, SM] + [VM] * (3 + len(deltas)),
        [shape(pre_shape, F32), shape(shifted, BF16), bricks_half] + outbound,
        [table],
        (send, nbr, x, mask, kernel_one, *x_in),
    )
    hidden_in = [from_behind(v, "space", d) for v, d in zip(sends, deltas)]
    (grad_one,) = call(
        inner_kernel,
        [SM] + [VM] * (4 + len(deltas)),
        [grads],
        [pltpu.VMEM((bricks + 1,) + brick, F32)],
        (send, mask, pre, windows, own_back, *back_in),
    )
    output, grad_two = call(
        second_kernel,
        [SM] + [VM] * (4 + len(deltas)),
        [bricks_half, grads],
        [table, pltpu.VMEM(shifted, BF16), pltpu.VMEM(pre_shape, F32)],
        (nbr, hidden, grad_out[0], mask, kernel_two, *hidden_in),
    )
    grad_one = lax.psum(grad_one, ("space", "rep"))
    grad_two = lax.psum(grad_two, ("space", "rep"))
    return (output.reshape(features.shape), grad_one, grad_two)


def solution(mesh):
    in_specs = (
        P("rep", ("groups", "space"), None, None, None),
        P(),
        P(),
        P("rep", ("groups", "space"), None, None, None),
        P("rep", ("groups", "space"), None),
        P("rep", ("groups", "space"), None, None),
        P("rep", ("groups", "space"), None),
    )
    out_specs = (
        P("rep", ("groups", "space"), None, None, None),
        P("groups", None, None),
        P("groups", None, None),
    )
    return jax.shard_map(
        per_device, mesh=mesh, in_specs=in_specs, out_specs=out_specs, check_vma=False
    )
```

profile of v0, /device:TPU:1, one launch (start us, length us, event | category | flops | bytes accessed | tf_op | source)
XLA Modules:
  0.0 223.5 jit_solution(12735282567461822914)
XLA Ops:
  10.6 1.3 collective-permute-start
  11.9 4.6 %collective-permute-start.1 = (bf16[2,8,8,512]{3,2,1,0:T(8,128)(2,1)S(1)}, bf16[2,8,8,512]{3,2,1,0:T(8,128)(2,1)S(1)}, u32[]{:S(2)}, u32[]{:S(2)}) collective-permute-start(bf16[2,8,8,512]{3,2,1,0:T(8,128)(2,1)S(1)} %get-tuple-element.36), channel_id=1, source_target_pairs={{0,2},{2,4},{4,6},{6,8},{8,10},{10,12},{12,14},{1,3},{3,5},{5,7},{... | collective-permute-start | bytes 393224 | tf_op jit(solution)/shard_map/ppermute | solution.py:21
  16.5 5.3 %collective-permute-start.2 = (bf16[2,8,8,512]{3,2,1,0:T(8,128)(2,1)S(1)}, bf16[2,8,8,512]{3,2,1,0:T(8,128)(2,1)S(1)}, u32[]{:S(2)}, u32[]{:S(2)}) collective-permute-start(bf16[2,8,8,512]{3,2,1,0:T(8,128)(2,1)S(1)} %get-tuple-element.37), channel_id=1, source_target_pairs={{0,6},{2,8},{4,10},{6,12},{8,14},{1,7},{3,9},{5,11},{7,13},{9,15},... | collective-permute-start | bytes 393224 | tf_op jit(solution)/shard_map/ppermute | solution.py:21
  21.8 1.5 collective-permute-start.3
  23.3 2.1 collective-permute-start.4
  27.4 8.2 %shard_map.97 = (f32[4,8,8,512]{3,2,1,0:T(8,128)S(1)}, bf16[2,8,8,512]{3,2,1,0:T(8,128)(2,1)S(1)}, bf16[2,8,8,512]{3,2,1,0:T(8,128)(2,1)S(1)}, bf16[2,8,8,512]{3...) custom-call(s32[4,27]{1,0:T(4,128)S(1)} %bitcast.27, ...), custom_call_target="tpu_custom_call" | custom-call | tf_op jit(solution)/shard_map/pallas_call | solution.py:258
  35.6 1.3 collective-permute-start.5
  37.0 1.3 collective-permute-start.6
  38.3 1.3 collective-permute-start.7
  39.6 2.3 %collective-permute-start.16 = (bf16[2,8,8,512]{3,2,1,0:T(8,128)(2,1)S(1)}, bf16[2,8,8,512]{3,2,1,0:T(8,128)(2,1)S(1)}, u32[]{:S(2)}, u32[]{:S(2)}) collective-permute-start(bf16[2,8,8,512]{3,2,1,0:T(8,128)(2,1)S(1)} %get-tuple-element.56), channel_id=1, source_target_pairs={{0,2},{2,4},{4,6},{6,8},{8,10},{10,12},{12,14},{1,3},{3,5},{5,7},{... | collective-permute-start | bytes 393224 | tf_op jit(solution)/shard_map/ppermute | solution.py:21
  41.9 1.3 collective-permute-start.17
  43.2 7.2 %collective-permute-done.5.rest_5_ = bf16[2,8,8,512]{3,2,1,0:T(8,128)(2,1)S(1)} collective-permute-done((bf16[2,8,8,512]{3,2,1,0:T(8,128)(2,1)S(1)}, bf16[2,8,8,512]{3,2,1,0:T(8,128)(2,1)S(1)}, u32[]{:S(2)}, u32[]{:S(2)}) %collective-permute-start.5) | collective-permute-done | bytes 131104 | tf_op jit(solution)/shard_map/ppermute | solution.py:21
  51.6 1.6 collective-permute-done.6.rest_6_
  54.5 1.3 collective-permute-start.20
  55.9 5.8 %collective-permute-start.21 = (bf16[2,8,8,512]{3,2,1,0:T(8,128)(2,1)S(1)}, bf16[2,8,8,512]{3,2,1,0:T(8,128)(2,1)S(1)}, u32[]{:S(2)}, u32[]{:S(2)}) collective-permute-start(bf16[2,8,8,512]{3,2,1,0:T(8,128)(2,1)S(1)} %get-tuple-element.61), channel_id=1, source_target_pairs={{0,10},{2,12},{4,14},{1,11},{3,13},{5,15},{16,26},{18,28},{20,30},... | collective-permute-start | bytes 393224 | tf_op jit(solution)/shard_map/ppermute | solution.py:21
  62.0 4.4 %shard_map.95 = (f32[8,32,512]{2,1,0:T(8,128)S(1)}, bf16[3,10,32,640]{3,2,1,0:T(8,128)(2,1)S(1)}, bf16[4,8,8,512]{3,2,1,0:T(8,128)(2,1)S(1)}, bf16[2,8,8,512]{3,...) custom-call(s32[8,2]{1,0:T(8,128)S(1)} %copy.12.send_ref, ...), custom_call_target="tpu_custom_call" | custom-call | tf_op jit(solution)/shard_map/pallas_call | solution.py:258
  66.4 2.5 %collective-permute-start.22 = (bf16[2,8,8,512]{3,2,1,0:T(8,128)(2,1)S(1)}, bf16[2,8,8,512]{3,2,1,0:T(8,128)(2,1)S(1)}, u32[]{:S(2)}, u32[]{:S(2)}) collective-permute-start(bf16[2,8,8,512]{3,2,1,0:T(8,128)(2,1)S(1)} %get-tuple-element.62), channel_id=1, source_target_pairs={{0,8},{2,10},{4,12},{6,14},{1,9},{3,11},{5,13},{7,15},{16,24},{18,... | collective-permute-start | bytes 393224 | tf_op jit(solution)/shard_map/ppermute | solution.py:21
  69.0 2.3 %collective-permute-start.23 = (bf16[2,8,8,512]{3,2,1,0:T(8,128)(2,1)S(1)}, bf16[2,8,8,512]{3,2,1,0:T(8,128)(2,1)S(1)}, u32[]{:S(2)}, u32[]{:S(2)}) collective-permute-start(bf16[2,8,8,512]{3,2,1,0:T(8,128)(2,1)S(1)} %get-tuple-element.63), channel_id=1, source_target_pairs={{0,6},{2,8},{4,10},{6,12},{8,14},{1,7},{3,9},{5,11},{7,13},{9,15},... | collective-permute-start | bytes 393224 | tf_op jit(solution)/shard_map/ppermute | solution.py:21
  71.3 1.6 collective-permute-done.19.rest_3_
  74.2 7.9 %collective-permute-start.9 = (bf16[2,8,8,512]{3,2,1,0:T(8,128)(2,1)S(1)}, bf16[2,8,8,512]{3,2,1,0:T(8,128)(2,1)S(1)}, u32[]{:S(2)}, u32[]{:S(2)}) collective-permute-start(bf16[2,8,8,512]{3,2,1,0:T(8,128)(2,1)S(1)} %get-tuple-element.45), channel_id=1, source_target_pairs={{0,2},{2,4},{4,6},{6,8},{8,10},{10,12},{12,14},{1,3},{3,5},{5,7},{... | collective-permute-start | bytes 393224 | tf_op jit(solution)/shard_map/ppermute | solution.py:21
  82.1 4.2 %collective-permute-start.10 = (bf16[2,8,8,512]{3,2,1,0:T(8,128)(2,1)S(1)}, bf16[2,8,8,512]{3,2,1,0:T(8,128)(2,1)S(1)}, u32[]{:S(2)}, u32[]{:S(2)}) collective-permute-start(bf16[2,8,8,512]{3,2,1,0:T(8,128)(2,1)S(1)} %get-tuple-element.46), channel_id=1, source_target_pairs={{0,6},{2,8},{4,10},{6,12},{8,14},{1,7},{3,9},{5,11},{7,13},{9,15},... | collective-permute-start | bytes 393224 | tf_op jit(solution)/shard_map/ppermute | solution.py:21
  86.4 1.3 collective-permute-start.11
  87.7 1.3 collective-permute-start.12
  89.0 1.3 collective-permute-start.13
  90.3 1.3 collective-permute-start.14
  91.6 1.3 collective-permute-start.15
  93.3 3.8 %shard_map.98 = f32[27,64,64]{2,1,0:T(8,128)} custom-call(s32[8,2]{1,0:T(8,128)S(1)} %copy.12.send_ref, f32[256,8]{1,0:T(8,128)S(1)} %bitcast.19, f32[8,32,512]{2,1,0:T(8,128)S(1)} %get-tuple-element.53.pre_ref, bf16[3,10,32,640]{3,2,1,0:T(8,128)(2,1)S(1)} %get-tuple-element.54.shifted_ref, f32[4,8,8,512]{3,2,1,0:T(8,128)S(1)} %get-tuple-element.55.own_ref, ...), custom_call_target="tpu_custom_call" | custom-call | tf_op jit(solution)/shard_map/pallas_call | solution.py:258
  97.1 3.7 %collective-permute-done.13.rest_5_ = bf16[2,8,8,512]{3,2,1,0:T(8,128)(2,1)S(1)} collective-permute-done((bf16[2,8,8,512]{3,2,1,0:T(8,128)(2,1)S(1)}, bf16[2,8,8,512]{3,2,1,0:T(8,128)(2,1)S(1)}, u32[]{:S(2)}, u32[]{:S(2)}) %collective-permute-start.13) | collective-permute-done | bytes 131104 | tf_op jit(solution)/shard_map/ppermute | solution.py:21
  100.8 9.1 %collective-permute-done.14.rest_6_ = bf16[2,8,8,512]{3,2,1,0:T(8,128)(2,1)S(1)} collective-permute-done((bf16[2,8,8,512]{3,2,1,0:T(8,128)(2,1)S(1)}, bf16[2,8,8,512]{3,2,1,0:T(8,128)(2,1)S(1)}, u32[]{:S(2)}, u32[]{:S(2)}) %collective-permute-start.14) | collective-permute-done | bytes 131104 | tf_op jit(solution)/shard_map/ppermute | solution.py:21
  109.8 6.9 %shard_map.96 = (bf16[4,8,8,512]{3,2,1,0:T(8,128)(2,1)}, f32[27,64,64]{2,1,0:T(8,128)}) custom-call(s32[4,27]{1,0:T(4,128)S(1)} %bitcast.29, bf16[4,8,8,512]{3,2,1,0:T(8,128)(2,1)S(1)} %get-tuple-element.43.hidden_ref, bf16[4,8,8,512]{3,2,1,0:T(8,128)(2,1)S(1)} %bitcast.25, f32[256,8]{1,0:T(8,128)S(1)} %bitcast.20, bf16[9,256,128]{2,1,0:T(8,128)(2,1)S(1)} %bitcast.23, ...), custom_call_target="tpu_custom_call" | custom-call | tf_op jit(solution)/shard_map/pallas_call | solution.py:258
  116.8 96.7 %all-reduce.9.cloned.1.call-done = (f32[27,64,64]{2,1,0:T(8,128)}, f32[27,64,64]{2,1,0:T(8,128)}) async-done(((f32[27,64,64]{2,1,0:T(8,128)}, f32[27,64,64]{2,1,0:T(8,128)}), (f32[27,64,64]{2,1,0:T(8,128)}, f32[27,64,64]{2,1,0:T(8,128)})) %all-reduce.9.cloned.1.call-update) | async-done | bytes 884752 | tf_op jit(solution)/shard_map/psum | solution.py:333
  213.5 2.3 %copy.18 = f32[27,64,64]{2,1,0:T(8,128)} copy(f32[27,64,64]{2,1,0:T(8,128)} %get-tuple-element.68) | data formatting | bytes 884736
  (47 shorter events, 10.9 us)
Async XLA Ops:
  7.2 206.3 %all-reduce.9.cloned.1.call-start = ((), (), s32[]{:S(2)}) async-start(), calls=%async_computation | async-start | bytes 3538944 | tf_op jit(solution)/shard_map/psum | solution.py:333
  8.8 1.0 copy-start.1
  10.6 25.0 %collective-permute-start = (bf16[2,8,8,512]{3,2,1,0:T(8,128)(2,1)S(1)}, bf16[2,8,8,512]{3,2,1,0:T(8,128)(2,1)S(1)}, u32[]{:S(2)}, u32[]{:S(2)}) collective-permute-start(bf16[2,8,8,512]{3,2,1,0:T(8,128)(2,1)S(1)} %get-tuple-element.35), channel_id=1, source_target_pairs={{2,0},{4,2},{6,4},{8,6},{10,8},{12,10},{14,12},{3,1},{5,3},{7,5},{... | collective-permute-start | bytes 393224 | tf_op jit(solution)/shard_map/ppermute | solution.py:21
  11.9 25.0 %collective-permute-start.1 = (bf16[2,8,8,512]{3,2,1,0:T(8,128)(2,1)S(1)}, bf16[2,8,8,512]{3,2,1,0:T(8,128)(2,1)S(1)}, u32[]{:S(2)}, u32[]{:S(2)}) collective-permute-start(bf16[2,8,8,512]{3,2,1,0:T(8,128)(2,1)S(1)} %get-tuple-element.36), channel_id=1, source_target_pairs={{0,2},{2,4},{4,6},{6,8},{8,10},{10,12},{12,14},{1,3},{3,5},{5,7},{... | collective-permute-start | bytes 393224 | tf_op jit(solution)/shard_map/ppermute | solution.py:21
  16.5 21.7 %collective-permute-start.2 = (bf16[2,8,8,512]{3,2,1,0:T(8,128)(2,1)S(1)}, bf16[2,8,8,512]{3,2,1,0:T(8,128)(2,1)S(1)}, u32[]{:S(2)}, u32[]{:S(2)}) collective-permute-start(bf16[2,8,8,512]{3,2,1,0:T(8,128)(2,1)S(1)} %get-tuple-element.37), channel_id=1, source_target_pairs={{0,6},{2,8},{4,10},{6,12},{8,14},{1,7},{3,9},{5,11},{7,13},{9,15},... | collective-permute-start | bytes 393224 | tf_op jit(solution)/shard_map/ppermute | solution.py:21
  21.8 17.7 %collective-permute-start.3 = (bf16[2,8,8,512]{3,2,1,0:T(8,128)(2,1)S(1)}, bf16[2,8,8,512]{3,2,1,0:T(8,128)(2,1)S(1)}, u32[]{:S(2)}, u32[]{:S(2)}) collective-permute-start(bf16[2,8,8,512]{3,2,1,0:T(8,128)(2,1)S(1)} %get-tuple-element.38), channel_id=1, source_target_pairs={{0,8},{2,10},{4,12},{6,14},{1,9},{3,11},{5,13},{7,15},{16,24},{18,... | collective-permute-start | bytes 393224 | tf_op jit(solution)/shard_map/ppermute | solution.py:21
  23.3 18.5 %collective-permute-start.4 = (bf16[2,8,8,512]{3,2,1,0:T(8,128)(2,1)S(1)}, bf16[2,8,8,512]{3,2,1,0:T(8,128)(2,1)S(1)}, u32[]{:S(2)}, u32[]{:S(2)}) collective-permute-start(bf16[2,8,8,512]{3,2,1,0:T(8,128)(2,1)S(1)} %get-tuple-element.39), channel_id=1, source_target_pairs={{0,10},{2,12},{4,14},{1,11},{3,13},{5,15},{16,26},{18,28},{20,30},... | collective-permute-start | bytes 393224 | tf_op jit(solution)/shard_map/ppermute | solution.py:21
  26.5 1.0 copy-start
  26.5 0.9 copy-start.2
  26.8 34.9 %copy-start.5 = (bf16[27,64,64]{2,1,0:T(8,128)(2,1)S(1)}, bf16[27,64,64]{2,1,0:T(8,128)(2,1)}, u32[]{:S(2)}) copy-start(bf16[27,64,64]{2,1,0:T(8,128)(2,1)} %param.8) | copy-start | bytes 663556
  35.6 14.7 %collective-permute-start.5 = (bf16[2,8,8,512]{3,2,1,0:T(8,128)(2,1)S(1)}, bf16[2,8,8,512]{3,2,1,0:T(8,128)(2,1)S(1)}, u32[]{:S(2)}, u32[]{:S(2)}) collective-permute-start(bf16[2,8,8,512]{3,2,1,0:T(8,128)(2,1)S(1)} %get-tuple-element.40), channel_id=1, source_target_pairs={{10,0},{12,2},{14,4},{11,1},{13,3},{15,5},{26,16},{28,18},{30,20},... | collective-permute-start | bytes 393224 | tf_op jit(solution)/shard_map/ppermute | solution.py:21
  37.0 16.3 %collective-permute-start.6 = (bf16[2,8,8,512]{3,2,1,0:T(8,128)(2,1)S(1)}, bf16[2,8,8,512]{3,2,1,0:T(8,128)(2,1)S(1)}, u32[]{:S(2)}, u32[]{:S(2)}) collective-permute-start(bf16[2,8,8,512]{3,2,1,0:T(8,128)(2,1)S(1)} %get-tuple-element.41), channel_id=1, source_target_pairs={{8,0},{10,2},{12,4},{14,6},{9,1},{11,3},{13,5},{15,7},{24,16},{26,... | collective-permute-start | bytes 393224 | tf_op jit(solution)/shard_map/ppermute | solution.py:21
  38.3 16.3 %collective-permute-start.7 = (bf16[2,8,8,512]{3,2,1,0:T(8,128)(2,1)S(1)}, bf16[2,8,8,512]{3,2,1,0:T(8,128)(2,1)S(1)}, u32[]{:S(2)}, u32[]{:S(2)}) collective-permute-start(bf16[2,8,8,512]{3,2,1,0:T(8,128)(2,1)S(1)} %get-tuple-element.42), channel_id=1, source_target_pairs={{6,0},{8,2},{10,4},{12,6},{14,8},{7,1},{9,3},{11,5},{13,7},{15,9},... | collective-permute-start | bytes 393224 | tf_op jit(solution)/shard_map/ppermute | solution.py:21
  39.6 16.3 %collective-permute-start.16 = (bf16[2,8,8,512]{3,2,1,0:T(8,128)(2,1)S(1)}, bf16[2,8,8,512]{3,2,1,0:T(8,128)(2,1)S(1)}, u32[]{:S(2)}, u32[]{:S(2)}) collective-permute-start(bf16[2,8,8,512]{3,2,1,0:T(8,128)(2,1)S(1)} %get-tuple-element.56), channel_id=1, source_target_pairs={{0,2},{2,4},{4,6},{6,8},{8,10},{10,12},{12,14},{1,3},{3,5},{5,7},{... | collective-permute-start | bytes 393224 | tf_op jit(solution)/shard_map/ppermute | solution.py:21
  41.9 24.6 %collective-permute-start.17 = (bf16[2,8,8,512]{3,2,1,0:T(8,128)(2,1)S(1)}, bf16[2,8,8,512]{3,2,1,0:T(8,128)(2,1)S(1)}, u32[]{:S(2)}, u32[]{:S(2)}) collective-permute-start(bf16[2,8,8,512]{3,2,1,0:T(8,128)(2,1)S(1)} %get-tuple-element.57), channel_id=1, source_target_pairs={{2,0},{4,2},{6,4},{8,6},{10,8},{12,10},{14,12},{3,1},{5,3},{7,5},{... | collective-permute-start | bytes 393224 | tf_op jit(solution)/shard_map/ppermute | solution.py:21
  50.3 18.6 %collective-permute-start.18 = (bf16[2,8,8,512]{3,2,1,0:T(8,128)(2,1)S(1)}, bf16[2,8,8,512]{3,2,1,0:T(8,128)(2,1)S(1)}, u32[]{:S(2)}, u32[]{:S(2)}) collective-permute-start(bf16[2,8,8,512]{3,2,1,0:T(8,128)(2,1)S(1)} %get-tuple-element.58), channel_id=1, source_target_pairs={{6,0},{8,2},{10,4},{12,6},{14,8},{7,1},{9,3},{11,5},{13,7},{15,9},... | collective-permute-start | bytes 393224 | tf_op jit(solution)/shard_map/ppermute | solution.py:21
  53.2 19.7 %collective-permute-start.19 = (bf16[2,8,8,512]{3,2,1,0:T(8,128)(2,1)S(1)}, bf16[2,8,8,512]{3,2,1,0:T(8,128)(2,1)S(1)}, u32[]{:S(2)}, u32[]{:S(2)}) collective-permute-start(bf16[2,8,8,512]{3,2,1,0:T(8,128)(2,1)S(1)} %get-tuple-element.59), channel_id=1, source_target_pairs={{8,0},{10,2},{12,4},{14,6},{9,1},{11,3},{13,5},{15,7},{24,16},{26,... | collective-permute-start | bytes 393224 | tf_op jit(solution)/shard_map/ppermute | solution.py:21
  54.5 19.7 %collective-permute-start.20 = (bf16[2,8,8,512]{3,2,1,0:T(8,128)(2,1)S(1)}, bf16[2,8,8,512]{3,2,1,0:T(8,128)(2,1)S(1)}, u32[]{:S(2)}, u32[]{:S(2)}) collective-permute-start(bf16[2,8,8,512]{3,2,1,0:T(8,128)(2,1)S(1)} %get-tuple-element.60), channel_id=1, source_target_pairs={{10,0},{12,2},{14,4},{11,1},{13,3},{15,5},{26,16},{28,18},{30,20},... | collective-permute-start | bytes 393224 | tf_op jit(solution)/shard_map/ppermute | solution.py:21
  55.9 26.3 %collective-permute-start.21 = (bf16[2,8,8,512]{3,2,1,0:T(8,128)(2,1)S(1)}, bf16[2,8,8,512]{3,2,1,0:T(8,128)(2,1)S(1)}, u32[]{:S(2)}, u32[]{:S(2)}) collective-permute-start(bf16[2,8,8,512]{3,2,1,0:T(8,128)(2,1)S(1)} %get-tuple-element.61), channel_id=1, source_target_pairs={{0,10},{2,12},{4,14},{1,11},{3,13},{5,15},{16,26},{18,28},{20,30},... | collective-permute-start | bytes 393224 | tf_op jit(solution)/shard_map/ppermute | solution.py:21
  62.0 30.9 %copy-start.3 = (bf16[27,64,64]{2,1,0:T(8,128)(2,1)S(1)}, bf16[27,64,64]{2,1,0:T(8,128)(2,1)}, u32[]{:S(2)}) copy-start(bf16[27,64,64]{2,1,0:T(8,128)(2,1)} %param.9) | copy-start | bytes 663556
  66.4 20.0 %collective-permute-start.22 = (bf16[2,8,8,512]{3,2,1,0:T(8,128)(2,1)S(1)}, bf16[2,8,8,512]{3,2,1,0:T(8,128)(2,1)S(1)}, u32[]{:S(2)}, u32[]{:S(2)}) collective-permute-start(bf16[2,8,8,512]{3,2,1,0:T(8,128)(2,1)S(1)} %get-tuple-element.62), channel_id=1, source_target_pairs={{0,8},{2,10},{4,12},{6,14},{1,9},{3,11},{5,13},{7,15},{16,24},{18,... | collective-permute-start | bytes 393224 | tf_op jit(solution)/shard_map/ppermute | solution.py:21
  69.0 18.7 %collective-permute-start.23 = (bf16[2,8,8,512]{3,2,1,0:T(8,128)(2,1)S(1)}, bf16[2,8,8,512]{3,2,1,0:T(8,128)(2,1)S(1)}, u32[]{:S(2)}, u32[]{:S(2)}) collective-permute-start(bf16[2,8,8,512]{3,2,1,0:T(8,128)(2,1)S(1)} %get-tuple-element.63), channel_id=1, source_target_pairs={{0,6},{2,8},{4,10},{6,12},{8,14},{1,7},{3,9},{5,11},{7,13},{9,15},... | collective-permute-start | bytes 393224 | tf_op jit(solution)/shard_map/ppermute | solution.py:21
  72.9 16.1 %collective-permute-start.8 = (bf16[2,8,8,512]{3,2,1,0:T(8,128)(2,1)S(1)}, bf16[2,8,8,512]{3,2,1,0:T(8,128)(2,1)S(1)}, u32[]{:S(2)}, u32[]{:S(2)}) collective-permute-start(bf16[2,8,8,512]{3,2,1,0:T(8,128)(2,1)S(1)} %get-tuple-element.44), channel_id=1, source_target_pairs={{2,0},{4,2},{6,4},{8,6},{10,8},{12,10},{14,12},{3,1},{5,3},{7,5},{... | collective-permute-start | bytes 393224 | tf_op jit(solution)/shard_map/ppermute | solution.py:21
  74.2 16.1 %collective-permute-start.9 = (bf16[2,8,8,512]{3,2,1,0:T(8,128)(2,1)S(1)}, bf16[2,8,8,512]{3,2,1,0:T(8,128)(2,1)S(1)}, u32[]{:S(2)}, u32[]{:S(2)}) collective-permute-start(bf16[2,8,8,512]{3,2,1,0:T(8,128)(2,1)S(1)} %get-tuple-element.45), channel_id=1, source_target_pairs={{0,2},{2,4},{4,6},{6,8},{8,10},{10,12},{12,14},{1,3},{3,5},{5,7},{... | collective-permute-start | bytes 393224 | tf_op jit(solution)/shard_map/ppermute | solution.py:21
  82.1 9.5 %collective-permute-start.10 = (bf16[2,8,8,512]{3,2,1,0:T(8,128)(2,1)S(1)}, bf16[2,8,8,512]{3,2,1,0:T(8,128)(2,1)S(1)}, u32[]{:S(2)}, u32[]{:S(2)}) collective-permute-start(bf16[2,8,8,512]{3,2,1,0:T(8,128)(2,1)S(1)} %get-tuple-element.46), channel_id=1, source_target_pairs={{0,6},{2,8},{4,10},{6,12},{8,14},{1,7},{3,9},{5,11},{7,13},{9,15},... | collective-permute-start | bytes 393224 | tf_op jit(solution)/shard_map/ppermute | solution.py:21
  86.4 10.7 %collective-permute-start.11 = (bf16[2,8,8,512]{3,2,1,0:T(8,128)(2,1)S(1)}, bf16[2,8,8,512]{3,2,1,0:T(8,128)(2,1)S(1)}, u32[]{:S(2)}, u32[]{:S(2)}) collective-permute-start(bf16[2,8,8,512]{3,2,1,0:T(8,128)(2,1)S(1)} %get-tuple-element.47), channel_id=1, source_target_pairs={{0,8},{2,10},{4,12},{6,14},{1,9},{3,11},{5,13},{7,15},{16,24},{18,... | collective-permute-start | bytes 393224 | tf_op jit(solution)/shard_map/ppermute | solution.py:21
  87.7 9.4 %collective-permute-start.12 = (bf16[2,8,8,512]{3,2,1,0:T(8,128)(2,1)S(1)}, bf16[2,8,8,512]{3,2,1,0:T(8,128)(2,1)S(1)}, u32[]{:S(2)}, u32[]{:S(2)}) collective-permute-start(bf16[2,8,8,512]{3,2,1,0:T(8,128)(2,1)S(1)} %get-tuple-element.48), channel_id=1, source_target_pairs={{0,10},{2,12},{4,14},{1,11},{3,13},{5,15},{16,26},{18,28},{20,30},... | collective-permute-start | bytes 393224 | tf_op jit(solution)/shard_map/ppermute | solution.py:21
  89.0 11.8 %collective-permute-start.13 = (bf16[2,8,8,512]{3,2,1,0:T(8,128)(2,1)S(1)}, bf16[2,8,8,512]{3,2,1,0:T(8,128)(2,1)S(1)}, u32[]{:S(2)}, u32[]{:S(2)}) collective-permute-start(bf16[2,8,8,512]{3,2,1,0:T(8,128)(2,1)S(1)} %get-tuple-element.49), channel_id=1, source_target_pairs={{10,0},{12,2},{14,4},{11,1},{13,3},{15,5},{26,16},{28,18},{30,20},... | collective-permute-start | bytes 393224 | tf_op jit(solution)/shard_map/ppermute | solution.py:21
  90.3 19.5 %collective-permute-start.14 = (bf16[2,8,8,512]{3,2,1,0:T(8,128)(2,1)S(1)}, bf16[2,8,8,512]{3,2,1,0:T(8,128)(2,1)S(1)}, u32[]{:S(2)}, u32[]{:S(2)}) collective-permute-start(bf16[2,8,8,512]{3,2,1,0:T(8,128)(2,1)S(1)} %get-tuple-element.50), channel_id=1, source_target_pairs={{8,0},{10,2},{12,4},{14,6},{9,1},{11,3},{13,5},{15,7},{24,16},{26,... | collective-permute-start | bytes 393224 | tf_op jit(solution)/shard_map/ppermute | solution.py:21
  91.6 18.2 %collective-permute-start.15 = (bf16[2,8,8,512]{3,2,1,0:T(8,128)(2,1)S(1)}, bf16[2,8,8,512]{3,2,1,0:T(8,128)(2,1)S(1)}, u32[]{:S(2)}, u32[]{:S(2)}) collective-permute-start(bf16[2,8,8,512]{3,2,1,0:T(8,128)(2,1)S(1)} %get-tuple-element.51), channel_id=1, source_target_pairs={{6,0},{8,2},{10,4},{12,6},{14,8},{7,1},{9,3},{11,5},{13,7},{15,9},... | collective-permute-start | bytes 393224 | tf_op jit(solution)/shard_map/ppermute | solution.py:21
  213.5 2.3 %copy-start.4 = (f32[27,64,64]{2,1,0:T(8,128)S(1)}, f32[27,64,64]{2,1,0:T(8,128)}, u32[]{:S(2)}) copy-start(f32[27,64,64]{2,1,0:T(8,128)} %get-tuple-element.69) | copy-start | bytes 1327108
Sparse Core Ops, SparseCore 0:
  116.9 96.4 all-reduce.8
where the time goes:
time: 226 us; the launch traced here: 223 us
  waiting for transfers between devices  120 us (53%)
  starting transfers between devices  56.7 us (25%)
  Pallas kernels  24.2 us (11%)
  between operations  14.5 us (6%)
  local copies, waits for them, and re-layouts  6.63 us (3%)
    psum x1, waiting for transfers between devices, per_device(): grad_one = lax.psum(grad_one, ('space', 'rep'))  96.7 us
    ppermute x24, starting transfers between devices, from_behind(): lax.ppermute(value, axis, [(source, source + steps) for source in range(i...  56.6 us
    pallas_call x5, Pallas kernels, call(): pl.pallas_call(body, out_shape=outs, in_specs=specs, out_specs=[VM] * len...  24.2 us
    ppermute x24, waiting for transfers between devices, from_behind(): lax.ppermute(value, axis, [(source, source + steps) for source in range(i...  23.1 us
  transfers between devices with their start and end apart: 25, of which 6 were waited for; matrix products, arithmetic and copies ran while one was open for 1% of the time, Pallas kernels for 7%

commit v1 on v0

--- a/solution.py
+++ b/solution.py
@@ -15,12 +15,6 @@
 SM = pl.BlockSpec(memory_space=pltpu.SMEM)
 
 
-def from_behind(value, axis, steps):
-    count = lax.axis_size(axis)
-    initial, last = (max(0, -steps), min(count, count - steps))
-    return lax.ppermute(value, axis, [(source, source + steps) for source in range(initial, last)])
-
-
 def iota(shape, dim):
     return lax.broadcasted_iota(jnp.int32, shape, dim)
 
@@ -37,22 +31,11 @@
     return jnp.concatenate([ref[b].astype(F32) for b in range(ref.shape[0])], axis=1)
 
 
-def fill_outbound(send_ref, bricks_ref, out_refs):
-    last = bricks_ref.shape[0] - 1
-    for k, out in enumerate(out_refs):
-        for s in range(out.shape[0]):
-            out[s] = bricks_ref[jnp.minimum(send_ref[k, s], last)]
-
-
-def fill_table(table_ref, own_ref, received):
-    bricks = own_ref.shape[0]
-    table_ref[0:bricks] = own_ref[...]
-    row = bricks
-    for ref in received:
-        count = ref.shape[0]
-        table_ref[row : row + count] = ref[...]
-        row += count
-    table_ref[row] = jnp.zeros(table_ref.shape[1:], table_ref.dtype)
+def fill_outbound(send_ref, bricks_ref, out_ref, bricks):
+    slots = send_ref.shape[1]
+    for k in range(send_ref.shape[0]):
+        for s in range(slots):
+            out_ref[slots * k + s] = bricks_ref[jnp.minimum(send_ref[k, s], bricks - 1)]
 
 
 def assemble(table_ref, nbr_ref, shifted_ref):
@@ -129,24 +112,18 @@
                 )
             flat = total.T
             for k in range(3):
-                grad_ref[9 * i + 3 * j + k] = (
+                block = (
                     flat[64 * k : 64 * k + 64, 0:64] + flat[64 * k + 64 : 64 * k + 128, 64:128]
                 )
+                at = pl.multiple_of(32 * (9 * i + 3 * j + k), 32)
+                grad_ref[pl.ds(at, 32), :] = jnp.concatenate([block[0:32], block[32:64]], axis=1)
         return carry
 
     lax.fori_loop(0, 3, step, 0)
 
 
-def mask_kernel(send_ref, features_ref, mask_ref, x_ref, *out_refs):
-    wide = expand_mask(mask_ref)
-    for b in range(x_ref.shape[0]):
-        part = wide[:, BE * b : BE * b + BE, :]
-        x_ref[b] = (features_ref[b].astype(F32) * part).astype(BF16)
-    fill_outbound(send_ref, x_ref, out_refs)
-
-
 def spread_kernel(nbr_ref, up_ref, mask_ref, kernel_ref, own_ref, *rest):
-    out_refs, (shifted_ref, spread_ref, totals_ref) = rest[:-3], rest[-3:]
+    out_ref, shifted_ref, spread_ref, totals_ref = rest
     bricks, width = own_ref.shape[0], own_ref.shape[3]
     wide = expand_mask(mask_ref)
     up = (to_rows(up_ref) * wide).astype(BF16).astype(F32)
@@ -198,53 +175,213 @@
 
     lax.fori_loop(0, BE + 2, deposit, 0)
     own_ref[...] = totals_ref[0:bricks]
-    row = bricks
-    for out in out_refs:
-        count = out.shape[0]
-        out[...] = totals_ref[row : row + count].astype(BF16)
-        row += count
-
-
-def first_kernel(count, send_ref, nbr_ref, x_ref, mask_ref, kernel_ref, *rest):
-    received, rest = rest[:count], rest[count:]
-    pre_ref, shifted_ref, hidden_ref = rest[:3]
-    out_refs, (table_ref,) = rest[3:-1], rest[-1:]
-    fill_table(table_ref, x_ref, received)
-    assemble(table_ref, nbr_ref, shifted_ref)
-    banded_conv(shifted_ref, kernel_ref, pre_ref)
+    out_ref[...] = totals_ref[bricks : bricks + out_ref.shape[0]].astype(BF16)
+
+
+def remote(source, target, sems, index, device):
+    return pltpu.make_async_remote_copy(
+        src_ref=source,
+        dst_ref=target,
+        send_sem=sems.at[0, index],
+        recv_sem=sems.at[1, index],
+        device_id=device,
+        device_id_type=pl.DeviceIdType.MESH,
+    )
+
+
+class Halo:
+    def __init__(self, owners, slots, sign, source, target, base, sems):
+        half = owners // 2
+        me = lax.axis_index("space")
+        row, column = me // half, me % half
+        self.sends, self.receives = [], []
+        steps = [(0, -1), (0, 1), (1, -1), (1, 0), (1, 1), (-1, -1), (-1, 0), (-1, 1)]
+        for k, (down, right) in enumerate(steps):
+            down, right = sign * down, sign * right
+            to_row, to_column = row + down, column + right
+            from_row, from_column = row - down, column - right
+            goes = (to_row >= 0) & (to_row < 2) & (to_column >= 0) & (to_column < half)
+            comes = (from_row >= 0) & (from_row < 2) & (from_column >= 0) & (from_column < half)
+            device = {"space": (me + down * half + right + owners) % owners}
+            copy = remote(
+                source.at[slots * k : slots * k + slots],
+                target.at[base + slots * k : base + slots * k + slots],
+                sems,
+                k,
+                device,
+            )
+            self.sends.append((goes, copy))
+            self.receives.append((comes, copy))
+
+    def start(self):
+        for goes, copy in self.sends:
+            pl.when(goes)(copy.start)
+
+    def wait_recv(self):
+        for comes, copy in self.receives:
+            pl.when(comes)(copy.wait_recv)
+
+    def wait_send(self):
+        for goes, copy in self.sends:
+            pl.when(goes)(copy.wait_send)
+
+
+class Total:
+    def __init__(self, owners, grad, pair_out, pair_in, mine, out, arrived, full, sems):
+        self.owners = owners
+        self.me = lax.axis_index("space")
+        self.rep = lax.axis_index("rep")
+        self.grad, self.pair_out, self.mine, self.out = grad, pair_out, mine, out
+        self.pair_in, self.arrived, self.full = pair_in, arrived, full
+        self.half = mine.shape[0]
+        self.chunk = self.half // owners
+        other = {"rep": 1 - self.rep}
+        self.pair = remote(pair_out, pair_in, sems, 0, other)
+        self.scatter, self.gather_out, self.gather_in = [], [], []
+        own = full.at[self.rep, self.rows(self.me), :]
+        for s in range(1, owners):
+            there = (self.me + s) % owners
+            device = {"space": there}
+            self.scatter.append(
+                remote(out.at[self.rows(there), :], arrived.at[s - 1], sems, s, device)
+            )
+            landing = full.at[self.rep, self.rows((self.me + owners - s) % owners), :]
+            index = owners + s
+            self.gather_out.append(remote(own, own, sems, index, device))
+            self.gather_in.append(remote(landing, landing, sems, index, device))
+        self.share = remote(full.at[self.rep], full.at[self.rep], sems, owners, other)
+        coming = full.at[1 - self.rep]
+        self.share_in = remote(coming, coming, sems, owners, other)
+
+    def rows(self, owner):
+        return pl.ds(pl.multiple_of(owner * self.chunk, self.chunk), self.chunk)
+
+    def halves(self, rep):
+        return pl.ds(pl.multiple_of(rep * self.half, self.half), self.half)
+
+    def start_pair(self):
+        self.pair_out[...] = self.grad[self.halves(1 - self.rep), :].astype(BF16)
+        self.pair.start()
+
+    def start_scatter(self):
+        self.pair.wait_recv()
+        total = self.grad[self.halves(self.rep), :] + self.pair_in[...].astype(F32)
+        self.mine[...] = total
+        self.out[...] = total.astype(BF16)
+        for copy in self.scatter:
+            copy.start()
+
+    def start_gather(self):
+        total = self.mine[self.rows(self.me), :]
+        for s, copy in enumerate(self.scatter):
+            copy.wait_recv()
+            total = total + self.arrived[s].astype(F32)
+        self.full[self.rep, self.rows(self.me), :] = total.astype(BF16)
+        for copy in self.gather_out:
+            copy.start()
+
+    def start_share(self):
+        for copy in self.gather_in:
+            copy.wait_recv()
+        self.share.start()
+
+    def finish(self, result_ref):
+        self.share_in.wait_recv()
+        flat = self.full[...].astype(F32).reshape(2 * self.half, 128)
+        for d in range(result_ref.shape[0]):
+            block = flat[32 * d : 32 * d + 32]
+            result_ref[d, 0:32, :] = block[:, 0:64]
+            result_ref[d, 32:64, :] = block[:, 64:128]
+        for copy in [self.pair, self.share] + self.scatter + self.gather_out:
+            copy.wait_send()
+
+
+def layers_kernel(
+    owners, send_ref, nbr_ref, features_ref, up_ref, mask_ref, one_ref, two_ref, own_ref, terms_ref,
+    output_ref, grad_one_ref, grad_two_ref,
+    x_table, x_out, hidden_table, hidden_out, terms_in, shifted_ref, pre_ref, wide_ref, home_ref,
+    bricks_ref, halo_sems, *rest
+):
+    bricks = own_ref.shape[0]
+    slots = send_ref.shape[1]
+    me, rep = lax.axis_index("space"), lax.axis_index("rep")
+    barrier = pltpu.get_barrier_semaphore()
+    mesh_id = pl.DeviceIdType.MESH
+    for s in range(1, owners):
+        there = {"space": (me + s) % owners}
+        pl.semaphore_signal(barrier, inc=1, device_id=there, device_id_type=mesh_id)
+    pl.semaphore_signal(barrier, inc=1, device_id={"rep": 1 - rep}, device_id_type=mesh_id)
+
+    x_halo = Halo(owners, slots, 1, x_out, x_table, bricks, halo_sems.at[0])
+    back_halo = Halo(owners, slots, -1, terms_ref, terms_in, 0, halo_sems.at[1])
+    hidden_halo = Halo(owners, slots, 1, hidden_out, hidden_table, bricks, halo_sems.at[2])
+    one, two = Total(owners, *rest[:8]), Total(owners, *rest[8:])
+
+    wide_ref[...] = expand_mask(mask_ref)
+    for b in range(bricks):
+        part = wide_ref[:, BE * b : BE * b + BE, :]
+        bricks_ref[b] = (features_ref[b].astype(F32) * part).astype(BF16)
+    x_table[0:bricks] = bricks_ref[...]
+    empty = jnp.zeros(x_table.shape[1:], BF16)
+    x_table[x_table.shape[0] - 1] = empty
+    hidden_table[x_table.shape[0] - 1] = empty
+    fill_outbound(send_ref, bricks_ref, x_out, bricks)
+    pl.semaphore_wait(barrier, owners)
+    x_halo.start()
+    back_halo.start()
+    for total in (one, two):
+        size = 32 * grad_one_ref.shape[0]
+        total.grad[size:, :] = jnp.zeros((total.grad.shape[0] - size, 128), F32)
+    x_halo.wait_recv()
+
+    assemble(x_table, nbr_ref, shifted_ref)
+    banded_conv(shifted_ref, one_ref, pre_ref)
     pre = pre_ref[...]
-    hidden = expand_mask(mask_ref) * (pre * jax.nn.sigmoid(pre))
-    for b in range(hidden_ref.shape[0]):
-        hidden_ref[b] = hidden[:, BE * b : BE * b + BE, :].astype(BF16)
-    fill_outbound(send_ref, hidden_ref, out_refs)
-
-
-def inner_kernel(send_ref, mask_ref, pre_ref, shifted_ref, own_ref, *rest):
-    received, (grad_ref, home_ref) = rest[:-2], rest[-2:]
-    bricks = own_ref.shape[0]
-    home_ref[0:bricks] = own_ref[...]
-    for k, ref in enumerate(received):
-        for s in range(ref.shape[0]):
-            home_ref[send_ref[k, s]] += ref[s].astype(F32)
+    hidden = wide_ref[...] * (pre * jax.nn.sigmoid(pre))
+    for b in range(bricks):
+        bricks_ref[b] = hidden[:, BE * b : BE * b + BE, :].astype(BF16)
+    hidden_table[0:bricks] = bricks_ref[...]
+    fill_outbound(send_ref, bricks_ref, hidden_out, bricks)
+    hidden_halo.start()
+
+    back_halo.wait_recv()
+    home_ref[...] = own_ref[...]
+    for k, (comes, unused) in enumerate(back_halo.receives):
+
+        @pl.when(comes)
+        def add_terms():
+            for s in range(slots):
+                term = terms_in[slots * k + s].astype(F32)
+                for b in range(bricks):
+                    home_ref[b] += jnp.where(send_ref[k, s] == b, term, 0.0)
+
     back = jnp.concatenate([home_ref[b] for b in range(bricks)], axis=1)
     pre = pre_ref[...]
     logistic = jax.nn.sigmoid(pre)
     slope = logistic * (1.0 + pre * (1.0 - logistic))
-    inner = (expand_mask(mask_ref) * back * slope).astype(BF16).astype(F32)
-    banded_grad(shifted_ref, inner.reshape(-1, inner.shape[2]), grad_ref)
-
-
-def second_kernel(nbr_ref, hidden_ref, up_ref, mask_ref, kernel_ref, *rest):
-    received, (output_ref, grad_ref, table_ref, shifted_ref, post_ref) = rest[:-5], rest[-5:]
-    fill_table(table_ref, hidden_ref, received)
-    assemble(table_ref, nbr_ref, shifted_ref)
-    wide = expand_mask(mask_ref)
-    up = (to_rows(up_ref) * wide).astype(BF16).astype(F32)
-    banded_grad(shifted_ref, up.reshape(-1, up.shape[2]), grad_ref)
-    banded_conv(shifted_ref, kernel_ref, post_ref)
-    post = post_ref[...] * wide
-    for b in range(output_ref.shape[0]):
+    inner = (wide_ref[...] * back * slope).astype(BF16).astype(F32)
+    banded_grad(shifted_ref, inner.reshape(-1, inner.shape[2]), one.grad)
+    one.start_pair()
+
+    hidden_halo.wait_recv()
+    assemble(hidden_table, nbr_ref, shifted_ref)
+    one.start_scatter()
+    up = (to_rows(up_ref) * wide_ref[...]).astype(BF16).astype(F32)
+    banded_grad(shifted_ref, up.reshape(-1, up.shape[2]), two.grad)
+    two.start_pair()
+    one.start_gather()
+    two.start_scatter()
+    banded_conv(shifted_ref, two_ref, pre_ref)
+    post = pre_ref[...] * wide_ref[...]
+    for b in range(bricks):
         output_ref[b] = post[:, BE * b : BE * b + BE, :].astype(BF16)
+    one.start_share()
+    two.start_gather()
+    one.finish(grad_one_ref)
+    two.start_share()
+    two.finish(grad_two_ref)
+    for halo in (x_halo, back_halo, hidden_halo):
+        halo.wait_send()
 
 
 def banded(weight):
@@ -254,14 +391,14 @@
     return jnp.concatenate([left, right], axis=-1).reshape(9, 256, 128)
 
 
-def call(body, specs, outs, scratch, args):
+def call(body, specs, outs, scratch, args, **params):
     return pl.pallas_call(
         body,
         out_shape=outs,
         in_specs=specs,
         out_specs=[VM] * len(outs),
         scratch_shapes=scratch,
-        compiler_params=pltpu.CompilerParams(vmem_limit_bytes=LIMIT),
+        compiler_params=pltpu.CompilerParams(vmem_limit_bytes=LIMIT, **params),
     )(*args)
 
 
@@ -273,8 +410,6 @@
     nbr = local_nbr[0]
     owners = lax.axis_size("space")
     slots = send.shape[1]
-    half = owners // 2
-    deltas = [-1, 1, half - 1, half, half + 1, -half - 1, -half, 1 - half]
     mask = active[0].reshape(bricks, BE, BE, BE).transpose(1, 0, 2, 3).reshape(-1, BE)
     mask = mask.astype(F32)
     kernel_one = banded(weight_one)
@@ -282,24 +417,15 @@
     kernel_back = banded(jnp.flip(weight_two, 0).transpose(0, 2, 1))
 
     shape = jax.ShapeDtypeStruct
-    outbound = [shape((slots,) + brick, BF16)] * len(deltas)
+    moved = send.shape[0] * slots
     bricks_half = shape((bricks,) + brick, BF16)
     bricks_full = shape((bricks,) + brick, F32)
-    entries = bricks + len(deltas) * slots + 1
+    entries = bricks + moved + 1
     rows = bricks * BE
-    table = pltpu.VMEM((entries,) + brick, BF16)
-    shifted = (3, BE + 2, rows, width + 128)
-    grads = shape(weight_one.shape, F32)
-    pre_shape = (BE, rows, width)
-
-    x, *sends = call(
-        mask_kernel, [SM, VM, VM], [bricks_half] + outbound, [], (send, features[0], mask)
-    )
-    x_in = [from_behind(v, "space", d) for v, d in zip(sends, deltas)]
-    own_back, *sends = call(
+    own_back, terms = call(
         spread_kernel,
         [SM, VM, VM, VM],
-        [bricks_full] + outbound,
+        [bricks_full, shape((moved,) + brick, BF16)],
         [
             pltpu.VMEM((3, BE + 4, 16 * bricks, width + 256), BF16),
             pltpu.VMEM((BE + 2, 16 * bricks, width + 128), F32),
@@ -307,31 +433,44 @@
         ],
         (nbr, grad_out[0], mask, kernel_back),
     )
-    back_in = [from_behind(v, "space", -d) for v, d in zip(sends, deltas)]
-    pre, windows, hidden, *sends = call(
-        functools.partial(first_kernel, len(deltas)),
-        [SM, SM] + [VM] * (3 + len(deltas)),
-        [shape(pre_shape, F32), shape(shifted, BF16), bricks_half] + outbound,
-        [table],
-        (send, nbr, x, mask, kernel_one, *x_in),
-    )
-    hidden_in = [from_behind(v, "space", d) for v, d in zip(sends, deltas)]
-    (grad_one,) = call(
-        inner_kernel,
-        [SM] + [VM] * (4 + len(deltas)),
-        [grads],
-        [pltpu.VMEM((bricks + 1,) + brick, F32)],
-        (send, mask, pre, windows, own_back, *back_in),
-    )
-    output, grad_two = call(
-        second_kernel,
-        [SM] + [VM] * (4 + len(deltas)),
-        [bricks_half, grads],
-        [table, pltpu.VMEM(shifted, BF16), pltpu.VMEM(pre_shape, F32)],
-        (nbr, hidden, grad_out[0], mask, kernel_two, *hidden_in),
-    )
-    grad_one = lax.psum(grad_one, ("space", "rep"))
-    grad_two = lax.psum(grad_two, ("space", "rep"))
+    grads = shape(weight_one.shape, F32)
+    chunk = -(-32 * weight_one.shape[0] // (2 * owners * 16)) * 16
+    half = owners * chunk
+    total = [
+        pltpu.VMEM((2 * half, 128), F32),
+        pltpu.VMEM((half, 128), BF16),
+        pltpu.VMEM((half, 128), BF16),
+        pltpu.VMEM((half, 128), F32),
+        pltpu.VMEM((half, 128), BF16),
+        pltpu.VMEM((owners - 1, chunk, 128), BF16),
+        pltpu.VMEM((2, half, 128), BF16),
+        pltpu.SemaphoreType.DMA((2, 2 * owners)),
+    ]
+    table = pltpu.VMEM((entries,) + brick, BF16)
+    outgoing = pltpu.VMEM((moved,) + brick, BF16)
+    output, grad_one, grad_two = call(
+        functools.partial(layers_kernel, owners),
+        [SM, SM] + [VM] * 7,
+        [bricks_half, grads, grads],
+        [
+            table,
+            outgoing,
+            table,
+            outgoing,
+            outgoing,
+            pltpu.VMEM((3, BE + 2, rows, width + 128), BF16),
+            pltpu.VMEM((BE, rows, width), F32),
+            pltpu.VMEM((BE, rows, width), F32),
+            pltpu.VMEM((bricks,) + brick, F32),
+            pltpu.VMEM((bricks,) + brick, BF16),
+            pltpu.SemaphoreType.DMA((3, 2, send.shape[0])),
+        ]
+        + total
+        + total,
+        (send, nbr, features[0], grad_out[0], mask, kernel_one, kernel_two, own_back, terms),
+        collective_id=0,
+        has_side_effects=True,
+    )
     return (output.reshape(features.shape), grad_one, grad_two)
 
 

time: 226 us -> 86 us (0.38)
  waiting for transfers between devices: 120 us -> 0 us
  starting transfers between devices: 56.7 us -> 0 us
  Pallas kernels: 24.2 us -> 78.2 us
  between operations: 14.5 us -> 0.76 us
    psum x1 -> x0, waiting for transfers between devices: 96.7 us -> none  [per_device(): grad_one = lax.psum(grad_one, ('space', 'rep'))]
    ppermute x24 -> x0, starting transfers between devices: 56.6 us -> none  [from_behind(): lax.ppermute(value, axis, [(source, source + steps) for source in range(i...]
    pallas_call x5 -> x2, Pallas kernels: 24.2 us -> 78.2 us  [call(): pl.pallas_call(body, out_shape=outs, in_specs=specs, out_specs=[VM] * len...]
    ppermute x24 -> x0, waiting for transfers between devices: 23.1 us -> none  [from_behind(): lax.ppermute(value, axis, [(source, source + steps) for source in range(i...]
  transfers between devices with their start and end apart: 25 -> 0, of which waited for: 6 -> 0; matrix products, arithmetic and copies ran while one was open for 1% -> 0% of each run, Pallas kernels for 7% -> 0%
where the time goes in v1:
time: 86 us; the launch traced here: 85.7 us
  Pallas kernels  78.2 us (91%)
  local copies, waits for them, and re-layouts  5.1 us (6%)
  other arithmetic  1.67 us (2%)
    pallas_call x2, Pallas kernels, call(): pl.pallas_call(body, out_shape=outs, in_specs=specs, out_specs=[VM] * len...  78.2 us
    unnamed x13, local copies, waits for them, and re-layouts  2.91 us

profile of v1, /device:TPU:1, one launch (start us, length us, event | category | flops | bytes accessed | tf_op | source)
XLA Modules:
  0.0 85.7 jit_solution(7617668250697080244)
XLA Ops:
  0.6 0.8 copy.13.send_ref
  1.4 0.7 convert_element_type.17
  2.1 0.1 convert_element_type.18
  2.2 1.0 %rev.4 = bf16[27,64,64]{2,1,0:T(8,128)(2,1)S(1)} reverse(bf16[27,64,64]{2,1,0:T(8,128)(2,1)} %param.9), dimensions={0} | reverse | bytes 442368 | tf_op jit(solution)/shard_map/jit(_flip)/rev | solution.py:417
  3.3 0.0 copy-start.4
  3.3 0.3 copy.11
  3.6 0.0 copy-start.3
  3.6 0.3 fusion.8
  3.9 0.0 copy-start
  3.9 0.0 copy-start.2
  3.9 0.4 copy-done.4
  4.3 0.3 fusion.6
  4.6 0.0 copy-start.1
  4.6 0.0 copy-done.3
  4.6 0.3 fusion.7
  5.0 0.0 copy-done
  5.0 0.0 copy-done.2
  5.0 8.3 %shard_map.94 = (f32[4,8,8,512]{3,2,1,0:T(8,128)S(1)}, bf16[16,8,8,512]{3,2,1,0:T(8,128)(2,1)S(1)}) custom-call(s32[4,27]{1,0:T(4,128)S(1)} %bitcast.25, bf16[4,8,8,512]{3,2,1,0:T(8,128)(2,1)S(1)} %bitcast.21, f32[256,8]{1,0:T(8,128)S(1)} %bitcast.19, bf16[9,256,128]{2,1,0:T(8,128)(2,1)S(1)} %bitcast.16), custom_call_target="tpu_custom_call" | custom-call | tf_op jit(solution)/shard_map/pallas_call | solution.py:395
  13.2 0.0 copy-done.1
  13.2 69.9 %shard_map.95 = (bf16[4,8,8,512]{3,2,1,0:T(8,128)(2,1)S(1)}, f32[27,64,64]{2,1,0:T(8,128)S(1)}, f32[27,64,64]{2,1,0:T(8,128)S(1)}) custom-call(s32[8,2]{1,0:T(8,128)S(1)} %copy.13.send_ref, s32[4,27]{1,0:T(4,128)S(1)} %bitcast.26, bf16[4,8,8,512]{3,2,1,0:T(8,128)(2,1)S(1)} %bitcast.23, bf16[4,8,8,512]{3,2,1,0:T(8,128)(2,1)S(1)} %bitcast.22, ...), custom_call_target="tpu_custom_call" | custom-call | tf_op jit(solution)/shard_map/pallas_call | solution.py:395
  83.2 0.7 copy.17
  83.9 0.9 %copy.18 = f32[27,64,64]{2,1,0:T(8,128)} copy(f32[27,64,64]{2,1,0:T(8,128)S(1)} %get-tuple-element.17) | data formatting | bytes 884736
  84.8 0.9 %copy.19 = f32[27,64,64]{2,1,0:T(8,128)} copy(f32[27,64,64]{2,1,0:T(8,128)S(1)} %get-tuple-element.18) | data formatting | bytes 884736
  (1 shorter events, 0.0 us)
Async XLA Ops:
  3.3 1.0 %copy-start.4 = (bf16[27,64,64]{2,1,0:T(8,128)(2,1)S(1)}, bf16[27,64,64]{2,1,0:T(8,128)(2,1)}, u32[]{:S(2)}) copy-start(bf16[27,64,64]{2,1,0:T(8,128)(2,1)} %param.8) | copy-start | bytes 663556
  3.6 1.1 %copy-start.3 = (bf16[27,64,64]{2,1,0:T(8,128)(2,1)S(1)}, bf16[27,64,64]{2,1,0:T(8,128)(2,1)}, u32[]{:S(2)}) copy-start(bf16[27,64,64]{2,1,0:T(8,128)(2,1)} %param.9) | copy-start | bytes 663556
  3.9 1.1 %copy-start = (bf16[1,4,8,8,512]{4,3,2,1,0:T(8,128)(2,1)S(1)}, bf16[1,4,8,8,512]{4,3,2,1,0:T(8,128)(2,1)}, u32[]{:S(2)}) copy-start(bf16[1,4,8,8,512]{4,3,2,1,0:T(8,128)(2,1)} %param.10) | copy-start | bytes 786436
  3.9 1.1 %copy-start.2 = (s32[1,4,27]{2,1,0:T(4,128)S(1)}, s32[1,4,27]{2,1,0:T(4,128)}, u32[]{:S(2)}) copy-start(s32[1,4,27]{2,1,0:T(4,128)} %param.13) | copy-start | bytes 1300
  4.6 8.6 %copy-start.1 = (bf16[1,4,8,8,512]{4,3,2,1,0:T(8,128)(2,1)S(1)}, bf16[1,4,8,8,512]{4,3,2,1,0:T(8,128)(2,1)}, u32[]{:S(2)}) copy-start(bf16[1,4,8,8,512]{4,3,2,1,0:T(8,128)(2,1)} %param.7) | copy-start | bytes 786436

commit v2 on v1

--- a/solution.py
+++ b/solution.py
@@ -29,6 +29,73 @@
 
 def to_rows(ref):
     return jnp.concatenate([ref[b].astype(F32) for b in range(ref.shape[0])], axis=1)
+
+
+def pack_shell(planes):
+    width = planes[0].shape[1]
+    quarter, middle = iota((BE, 128), 1), width // 2
+    rows, rows_short = iota((BE, width), 0), iota((BE, middle), 0)
+
+    def gather(pairs):
+        out = jnp.zeros((BE, width), F32)
+        for r, (x, y) in enumerate(pairs):
+            out = jnp.where(rows == r, planes[x][y : y + 1, :], out)
+        return out
+
+    ends = [
+        jnp.where(quarter < 64, p[:, 0:128], p[:, width - 128 :]) for p in planes[1 : BE - 1]
+    ]
+    edge = [(x, y) for x in range(1, BE - 1) for y in (0, BE - 1)]
+    left = gather(edge[BE:])
+    spare = jnp.where(rows_short < 4, left[:, :middle], pltpu.roll(left[:, middle:], 4, 0))
+    third = jnp.concatenate(ends[:4], axis=1)
+    fourth = jnp.concatenate(ends[4:] + [spare], axis=1)
+    return [planes[0], planes[BE - 1], third, fourth, gather(edge[:BE])]
+
+
+def unpack_shell(tiles):
+    width = tiles[0].shape[1]
+    quarter, middle = iota((BE, 128), 1), width // 2
+    rows = iota((BE, width), 0)
+    spare = tiles[3][:, middle:]
+    left = jnp.concatenate([spare, pltpu.roll(spare, 4, 0)], axis=1)
+    ends = [tiles[2][:, 128 * q : 128 * q + 128] for q in range(4)]
+    ends += [tiles[3][:, 128 * q : 128 * q + 128] for q in range(2)]
+    planes = [tiles[0]]
+    for q, end in enumerate(ends):
+        source, r = (tiles[4], 2 * q) if q < 4 else (left, 2 * q - BE)
+        low = jnp.where(quarter < 64, end, 0.0)
+        high = jnp.where(quarter >= 64, end, 0.0)
+        plane = jnp.concatenate([low, jnp.zeros((BE, width - 256), F32), high], axis=1)
+        plane = jnp.where(rows == 0, source[r : r + 1, :], plane)
+        planes.append(jnp.where(rows == BE - 1, source[r + 1 : r + 2, :], plane))
+    return planes + [tiles[1]]
+
+
+def pack_bricks(source_ref, base, packed_ref):
+    def step(t, carry):
+        tiles = pack_shell([source_ref[base + t, x].astype(F32) for x in range(BE)])
+        for q, tile in enumerate(tiles):
+            packed_ref[t, q] = tile.astype(BF16)
+        return carry
+
+    lax.fori_loop(0, packed_ref.shape[0], step, 0)
+
+
+def unpack_arrived(halo, slots, landing_ref, table_ref, base):
+    for k, (comes, copy) in enumerate(halo.receives):
+
+        @pl.when(comes)
+        def unpack():
+            copy.wait_recv()
+
+            def step(t, carry):
+                tiles = [landing_ref[t, q].astype(F32) for q in range(5)]
+                for x, plane in enumerate(unpack_shell(tiles)):
+                    table_ref[base + t, x] = plane.astype(BF16)
+                return carry
+
+            lax.fori_loop(slots * k, slots * k + slots, step, 0)
 
 
 def fill_outbound(send_ref, bricks_ref, out_ref, bricks):
@@ -175,7 +242,7 @@
 
     lax.fori_loop(0, BE + 2, deposit, 0)
     own_ref[...] = totals_ref[0:bricks]
-    out_ref[...] = totals_ref[bricks : bricks + out_ref.shape[0]].astype(BF16)
+    pack_bricks(totals_ref, bricks, out_ref)
 
 
 def remote(source, target, sems, index, device):
@@ -216,10 +283,6 @@
     def start(self):
         for goes, copy in self.sends:
             pl.when(goes)(copy.start)
-
-    def wait_recv(self):
-        for comes, copy in self.receives:
-            pl.when(comes)(copy.wait_recv)
 
     def wait_send(self):
         for goes, copy in self.sends:
@@ -299,7 +362,7 @@
 def layers_kernel(
     owners, send_ref, nbr_ref, features_ref, up_ref, mask_ref, one_ref, two_ref, own_ref, terms_ref,
     output_ref, grad_one_ref, grad_two_ref,
-    x_table, x_out, hidden_table, hidden_out, terms_in, shifted_ref, pre_ref, wide_ref, home_ref,
+    table_ref, x_out, x_in, hidden_out, hidden_in, terms_in, packed_ref, shifted_ref, pre_ref, wide_ref, home_ref,
     bricks_ref, halo_sems, *rest
 ):
     bricks = own_ref.shape[0]
@@ -312,48 +375,53 @@
         pl.semaphore_signal(barrier, inc=1, device_id=there, device_id_type=mesh_id)
     pl.semaphore_signal(barrier, inc=1, device_id={"rep": 1 - rep}, device_id_type=mesh_id)
 
-    x_halo = Halo(owners, slots, 1, x_out, x_table, bricks, halo_sems.at[0])
+    x_halo = Halo(owners, slots, 1, x_out, x_in, 0, halo_sems.at[0])
     back_halo = Halo(owners, slots, -1, terms_ref, terms_in, 0, halo_sems.at[1])
-    hidden_halo = Halo(owners, slots, 1, hidden_out, hidden_table, bricks, halo_sems.at[2])
+    hidden_halo = Halo(owners, slots, 1, hidden_out, hidden_in, 0, halo_sems.at[2])
     one, two = Total(owners, *rest[:8]), Total(owners, *rest[8:])
 
     wide_ref[...] = expand_mask(mask_ref)
     for b in range(bricks):
         part = wide_ref[:, BE * b : BE * b + BE, :]
         bricks_ref[b] = (features_ref[b].astype(F32) * part).astype(BF16)
-    x_table[0:bricks] = bricks_ref[...]
-    empty = jnp.zeros(x_table.shape[1:], BF16)
-    x_table[x_table.shape[0] - 1] = empty
-    hidden_table[x_table.shape[0] - 1] = empty
-    fill_outbound(send_ref, bricks_ref, x_out, bricks)
+    table_ref[0:bricks] = bricks_ref[...]
+    table_ref[table_ref.shape[0] - 1] = jnp.zeros(table_ref.shape[1:], BF16)
+    pack_bricks(bricks_ref, 0, packed_ref)
+    fill_outbound(send_ref, packed_ref, x_out, bricks)
     pl.semaphore_wait(barrier, owners)
     x_halo.start()
     back_halo.start()
     for total in (one, two):
         size = 32 * grad_one_ref.shape[0]
         total.grad[size:, :] = jnp.zeros((total.grad.shape[0] - size, 128), F32)
-    x_halo.wait_recv()
-
-    assemble(x_table, nbr_ref, shifted_ref)
+    unpack_arrived(x_halo, slots, x_in, table_ref, bricks)
+
+    assemble(table_ref, nbr_ref, shifted_ref)
     banded_conv(shifted_ref, one_ref, pre_ref)
     pre = pre_ref[...]
     hidden = wide_ref[...] * (pre * jax.nn.sigmoid(pre))
     for b in range(bricks):
         bricks_ref[b] = hidden[:, BE * b : BE * b + BE, :].astype(BF16)
-    hidden_table[0:bricks] = bricks_ref[...]
-    fill_outbound(send_ref, bricks_ref, hidden_out, bricks)
+    pack_bricks(bricks_ref, 0, packed_ref)
+    fill_outbound(send_ref, packed_ref, hidden_out, bricks)
     hidden_halo.start()
-
-    back_halo.wait_recv()
+    table_ref[0:bricks] = bricks_ref[...]
+
     home_ref[...] = own_ref[...]
-    for k, (comes, unused) in enumerate(back_halo.receives):
+    for k, (comes, copy) in enumerate(back_halo.receives):
 
         @pl.when(comes)
         def add_terms():
-            for s in range(slots):
-                term = terms_in[slots * k + s].astype(F32)
-                for b in range(bricks):
-                    home_ref[b] += jnp.where(send_ref[k, s] == b, term, 0.0)
+            copy.wait_recv()
+
+            def step(s, carry):
+                tiles = [terms_in[slots * k + s, q].astype(F32) for q in range(5)]
+                for x, plane in enumerate(unpack_shell(tiles)):
+                    for b in range(bricks):
+                        home_ref[b, x] += jnp.where(send_ref[k, s] == b, plane, 0.0)
+                return carry
+
+            lax.fori_loop(0, slots, step, 0)
 
     back = jnp.concatenate([home_ref[b] for b in range(bricks)], axis=1)
     pre = pre_ref[...]
@@ -363,8 +431,8 @@
     banded_grad(shifted_ref, inner.reshape(-1, inner.shape[2]), one.grad)
     one.start_pair()
 
-    hidden_halo.wait_recv()
-    assemble(hidden_table, nbr_ref, shifted_ref)
+    unpack_arrived(hidden_halo, slots, hidden_in, table_ref, bricks)
+    assemble(table_ref, nbr_ref, shifted_ref)
     one.start_scatter()
     up = (to_rows(up_ref) * wide_ref[...]).astype(BF16).astype(F32)
     banded_grad(shifted_ref, up.reshape(-1, up.shape[2]), two.grad)
@@ -418,6 +486,7 @@
 
     shape = jax.ShapeDtypeStruct
     moved = send.shape[0] * slots
+    shell = (5, BE, width)
     bricks_half = shape((bricks,) + brick, BF16)
     bricks_full = shape((bricks,) + brick, F32)
     entries = bricks + moved + 1
@@ -425,7 +494,7 @@
     own_back, terms = call(
         spread_kernel,
         [SM, VM, VM, VM],
-        [bricks_full, shape((moved,) + brick, BF16)],
+        [bricks_full, shape((moved,) + shell, BF16)],
         [
             pltpu.VMEM((3, BE + 4, 16 * bricks, width + 256), BF16),
             pltpu.VMEM((BE + 2, 16 * bricks, width + 128), F32),
@@ -447,17 +516,19 @@
         pltpu.SemaphoreType.DMA((2, 2 * owners)),
     ]
     table = pltpu.VMEM((entries,) + brick, BF16)
-    outgoing = pltpu.VMEM((moved,) + brick, BF16)
+    moving = pltpu.VMEM((moved,) + shell, BF16)
     output, grad_one, grad_two = call(
         functools.partial(layers_kernel, owners),
         [SM, SM] + [VM] * 7,
         [bricks_half, grads, grads],
         [
             table,
-            outgoing,
-            table,
-            outgoing,
-            outgoing,
+            moving,
+            moving,
+            moving,
+            moving,
+            moving,
+            pltpu.VMEM((bricks,) + shell, BF16),
             pltpu.VMEM((3, BE + 2, rows, width + 128), BF16),
             pltpu.VMEM((BE, rows, width), F32),
             pltpu.VMEM((BE, rows, width), F32),

time: 86 us -> 70.2 us (0.82)
  Pallas kernels: 78.2 us -> 61.8 us
    pallas_call x2, Pallas kernels: 78.2 us -> 61.8 us  [call(): pl.pallas_call(body, out_shape=outs, in_specs=specs, out_specs=[VM] * len...]
where the time goes in v2:
time: 70.2 us; the launch traced here: 69.6 us
  Pallas kernels  61.8 us (88%)
  local copies, waits for them, and re-layouts  5.41 us (8%)
  other arithmetic  1.67 us (2%)
  between operations  0.73 us (1%)
    pallas_call x2, Pallas kernels, call(): pl.pallas_call(body, out_shape=outs, in_specs=specs, out_specs=[VM] * len...  61.8 us
    unnamed x13, local copies, waits for them, and re-layouts  3.22 us

profile of v2, /device:TPU:1, one launch (start us, length us, event | category | flops | bytes accessed | tf_op | source)
XLA Modules:
  0.0 69.6 jit_solution(7374853936933509949)
XLA Ops:
  0.6 0.8 %copy.13.send_ref = s32[8,2]{1,0:T(8,128)S(1)} copy(s32[8,2]{0,1:T(2,128)} %bitcast.30) | data formatting | bytes 128 | tf_op jit(solution)/shard_map/squeeze | solution.py:477
  1.4 0.7 %convert_element_type.17 = f32[1,4,512]{2,1,0:T(4,128)S(1)} convert(s32[1,4,512]{2,1,0:T(4,128)} %param.11) | non-fusion elementwise | flops 2048 | bytes 16384 | tf_op jit(solution)/shard_map/convert_element_type | solution.py:482
  2.1 0.1 convert_element_type.18
  2.2 1.0 %rev.4 = bf16[27,64,64]{2,1,0:T(8,128)(2,1)S(1)} reverse(bf16[27,64,64]{2,1,0:T(8,128)(2,1)} %param.9), dimensions={0} | reverse | bytes 442368 | tf_op jit(solution)/shard_map/jit(_flip)/rev | solution.py:485
  3.3 0.0 copy-start.4
  3.3 0.3 copy.11
  3.6 0.0 copy-start.3
  3.6 0.3 fusion.8
  3.9 0.4 copy-done.4
  4.3 0.0 copy-start
  4.3 0.0 copy-start.2
  4.3 0.3 fusion.6
  4.6 0.0 copy-done.3
  4.6 0.0 copy-start.1
  4.6 0.3 fusion.7
  5.0 0.3 copy-done
  5.3 0.0 copy-done.2
  5.3 8.4 %shard_map.94 = (f32[4,8,8,512]{3,2,1,0:T(8,128)S(1)}, bf16[16,5,8,512]{3,2,1,0:T(8,128)(2,1)S(1)}) custom-call(s32[4,27]{1,0:T(4,128)S(1)} %bitcast.25, bf16[4,8,8,512]{3,2,1,0:T(8,128)(2,1)S(1)} %bitcast.21, f32[256,8]{1,0:T(8,128)S(1)} %bitcast.19, bf16[9,256,128]{2,1,0:T(8,128)(2,1)S(1)} %bitcast.18), custom_call_target="tpu_custom_call" | custom-call | tf_op jit(solution)/shard_map/pallas_call | solution.py:463
  13.7 0.0 copy-done.1
  13.7 53.4 %shard_map.95 = (bf16[4,8,8,512]{3,2,1,0:T(8,128)(2,1)S(1)}, f32[27,64,64]{2,1,0:T(8,128)S(1)}, f32[27,64,64]{2,1,0:T(8,128)S(1)}) custom-call(s32[8,2]{1,0:T(8,128)S(1)} %copy.13.send_ref, s32[4,27]{1,0:T(4,128)S(1)} %bitcast.26, bf16[4,8,8,512]{3,2,1,0:T(8,128)(2,1)S(1)} %bitcast.23, bf16[4,8,8,512]{3,2,1,0:T(8,128)(2,1)S(1)} %bitcast.22, ...), custom_call_target="tpu_custom_call" | custom-call | tf_op jit(solution)/shard_map/pallas_call | solution.py:463
  67.1 0.7 %copy.17 = bf16[1,4,8,8,512]{4,3,2,1,0:T(8,128)(2,1)} copy(bf16[1,4,8,8,512]{4,3,2,1,0:T(8,128)(2,1)S(1)} %bitcast.24) | data formatting | bytes 524288
  67.8 0.9 %copy.18 = f32[27,64,64]{2,1,0:T(8,128)} copy(f32[27,64,64]{2,1,0:T(8,128)S(1)} %get-tuple-element.17) | data formatting | bytes 884736
  68.7 0.9 %copy.19 = f32[27,64,64]{2,1,0:T(8,128)} copy(f32[27,64,64]{2,1,0:T(8,128)S(1)} %get-tuple-element.18) | data formatting | bytes 884736
  (1 shorter events, 0.0 us)
Async XLA Ops:
  3.3 1.0 %copy-start.4 = (bf16[27,64,64]{2,1,0:T(8,128)(2,1)S(1)}, bf16[27,64,64]{2,1,0:T(8,128)(2,1)}, u32[]{:S(2)}) copy-start(bf16[27,64,64]{2,1,0:T(8,128)(2,1)} %param.8) | copy-start | bytes 663556
  3.6 1.1 %copy-start.3 = (bf16[27,64,64]{2,1,0:T(8,128)(2,1)S(1)}, bf16[27,64,64]{2,1,0:T(8,128)(2,1)}, u32[]{:S(2)}) copy-start(bf16[27,64,64]{2,1,0:T(8,128)(2,1)} %param.9) | copy-start | bytes 663556
  4.3 1.0 %copy-start = (bf16[1,4,8,8,512]{4,3,2,1,0:T(8,128)(2,1)S(1)}, bf16[1,4,8,8,512]{4,3,2,1,0:T(8,128)(2,1)}, u32[]{:S(2)}) copy-start(bf16[1,4,8,8,512]{4,3,2,1,0:T(8,128)(2,1)} %param.10) | copy-start | bytes 786436
  4.3 1.0 %copy-start.2 = (s32[1,4,27]{2,1,0:T(4,128)S(1)}, s32[1,4,27]{2,1,0:T(4,128)}, u32[]{:S(2)}) copy-start(s32[1,4,27]{2,1,0:T(4,128)} %param.13) | copy-start | bytes 1300
  4.6 9.0 %copy-start.1 = (bf16[1,4,8,8,512]{4,3,2,1,0:T(8,128)(2,1)S(1)}, bf16[1,4,8,8,512]{4,3,2,1,0:T(8,128)(2,1)}, u32[]{:S(2)}) copy-start(bf16[1,4,8,8,512]{4,3,2,1,0:T(8,128)(2,1)} %param.7) | copy-start | bytes 786436

commit v3 on v2

--- a/solution.py
+++ b/solution.py
@@ -23,7 +23,7 @@
     rows, edge = mask_ref.shape
     width = edge * 64
     spread = (iota((edge, width), 1) // 64 == iota((edge, width), 0)).astype(BF16)
-    wide = jnp.dot(mask_ref[...].astype(BF16), spread, preferred_element_type=F32)
+    wide = jnp.dot(mask_ref[...].astype(F32).astype(BF16), spread, preferred_element_type=F32)
     return wide.reshape(BE, rows // BE, width)
 
 
@@ -143,7 +143,25 @@
     lax.fori_loop(0, BE + 2, step, 0)
 
 
-def banded_conv(shifted_ref, kernel_ref, result_ref):
+def band_forward(weight_ref, kernel_ref):
+    empty = jnp.zeros((64, 64), F32)
+    for n in range(9):
+        three = [weight_ref[3 * n + k].astype(F32) for k in range(3)]
+        left = jnp.concatenate(three + [empty], axis=0)
+        right = jnp.concatenate([empty] + three, axis=0)
+        kernel_ref[n] = jnp.concatenate([left, right], axis=1).astype(BF16)
+
+
+def band_backward(weight_ref, kernel_ref):
+    empty = jnp.zeros((64, 64), F32)
+    for n in range(9):
+        three = [weight_ref[26 - 3 * n - k].astype(F32) for k in range(3)]
+        top = jnp.concatenate(three + [empty], axis=1)
+        low = jnp.concatenate([empty] + three, axis=1)
+        kernel_ref[n] = jnp.concatenate([top, low], axis=0).astype(BF16)
+
+
+def banded_conv(shifted_ref, kernel_ref, result_ref, first=0, last=None, turned=False):
     length, rows, width = result_ref.shape
 
     def step(p, carry):
@@ -152,15 +170,16 @@
         for i in range(3):
             for j in range(3):
                 block = shifted_ref[j, i : i + length, :, pl.ds(at, 256)]
-                total = total + jnp.dot(
+                total = total + lax.dot_general(
                     block.reshape(length * rows, 256),
                     kernel_ref[3 * i + j],
+                    (((1,), (1 if turned else 0,)), ((), ())),
                     preferred_element_type=F32,
                 )
         result_ref[:, :, pl.ds(at, 128)] = total.reshape(length, rows, 128)
         return carry
 
-    lax.fori_loop(0, width // 128, step, 0)
+    lax.fori_loop(first, width // 128 if last is None else last, step, 0)
 
 
 def banded_grad(shifted_ref, upward, grad_ref):
@@ -189,8 +208,9 @@
     lax.fori_loop(0, 3, step, 0)
 
 
-def spread_kernel(nbr_ref, up_ref, mask_ref, kernel_ref, own_ref, *rest):
-    out_ref, shifted_ref, spread_ref, totals_ref = rest
+def spread_kernel(nbr_ref, up_ref, mask_ref, weight_ref, own_ref, *rest):
+    out_ref, shifted_ref, spread_ref, totals_ref, kernel_ref = rest
+    band_backward(weight_ref, kernel_ref)
     bricks, width = own_ref.shape[0], own_ref.shape[3]
     wide = expand_mask(mask_ref)
     up = (to_rows(up_ref) * wide).astype(BF16).astype(F32)
@@ -206,7 +226,7 @@
             for j in range(3):
                 moved = pltpu.roll(tile, 2 - j, 0) if j < 2 else tile
                 shifted_ref[j, x + 2, 16 * b : 16 * b + 16, :] = moved.astype(BF16)
-    banded_conv(shifted_ref, kernel_ref, spread_ref)
+    banded_conv(shifted_ref, kernel_ref, spread_ref, turned=True)
 
     def clear(t, carry):
         totals_ref[t] = jnp.zeros(totals_ref.shape[1:], F32)
@@ -363,7 +383,7 @@
     owners, send_ref, nbr_ref, features_ref, up_ref, mask_ref, one_ref, two_ref, own_ref, terms_ref,
     output_ref, grad_one_ref, grad_two_ref,
     table_ref, x_out, x_in, hidden_out, hidden_in, terms_in, packed_ref, shifted_ref, pre_ref, wide_ref, home_ref,
-    bricks_ref, halo_sems, *rest
+    bricks_ref, kernel_ref, halo_sems, *rest
 ):
     bricks = own_ref.shape[0]
     slots = send_ref.shape[1]
@@ -394,10 +414,12 @@
     for total in (one, two):
         size = 32 * grad_one_ref.shape[0]
         total.grad[size:, :] = jnp.zeros((total.grad.shape[0] - size, 128), F32)
+    band_forward(one_ref, kernel_ref.at[0])
+    band_forward(two_ref, kernel_ref.at[1])
     unpack_arrived(x_halo, slots, x_in, table_ref, bricks)
 
     assemble(table_ref, nbr_ref, shifted_ref)
-    banded_conv(shifted_ref, one_ref, pre_ref)
+    banded_conv(shifted_ref, kernel_ref.at[0], pre_ref)
     pre = pre_ref[...]
     hidden = wide_ref[...] * (pre * jax.nn.sigmoid(pre))
     for b in range(bricks):
@@ -438,25 +460,20 @@
     banded_grad(shifted_ref, up.reshape(-1, up.shape[2]), two.grad)
     two.start_pair()
     one.start_gather()
+    banded_conv(shifted_ref, kernel_ref.at[1], pre_ref, 0, 1)
     two.start_scatter()
-    banded_conv(shifted_ref, two_ref, pre_ref)
+    banded_conv(shifted_ref, kernel_ref.at[1], pre_ref, 1, 3)
+    one.start_share()
+    two.start_gather()
+    banded_conv(shifted_ref, kernel_ref.at[1], pre_ref, 3, 4)
     post = pre_ref[...] * wide_ref[...]
     for b in range(bricks):
         output_ref[b] = post[:, BE * b : BE * b + BE, :].astype(BF16)
-    one.start_share()
-    two.start_gather()
     one.finish(grad_one_ref)
     two.start_share()
     two.finish(grad_two_ref)
     for halo in (x_halo, back_halo, hidden_halo):
         halo.wait_send()
-
-
-def banded(weight):
-    split = weight.reshape(9, 3, 64, 64)
-    left = jnp.pad(split, ((0, 0), (0, 1), (0, 0), (0, 0)))
-    right = jnp.pad(split, ((0, 0), (1, 0), (0, 0), (0, 0)))
-    return jnp.concatenate([left, right], axis=-1).reshape(9, 256, 128)
 
 
 def call(body, specs, outs, scratch, args, **params):
@@ -479,11 +496,6 @@
     owners = lax.axis_size("space")
     slots = send.shape[1]
     mask = active[0].reshape(bricks, BE, BE, BE).transpose(1, 0, 2, 3).reshape(-1, BE)
-    mask = mask.astype(F32)
-    kernel_one = banded(weight_one)
-    kernel_two = banded(weight_two)
-    kernel_back = banded(jnp.flip(weight_two, 0).transpose(0, 2, 1))
-
     shape = jax.ShapeDtypeStruct
     moved = send.shape[0] * slots
     shell = (5, BE, width)
@@ -499,8 +511,9 @@
             pltpu.VMEM((3, BE + 4, 16 * bricks, width + 256), BF16),
             pltpu.VMEM((BE + 2, 16 * bricks, width + 128), F32),
             pltpu.VMEM((entries,) + brick, F32),
+            pltpu.VMEM((9, 128, 256), BF16),
         ],
-        (nbr, grad_out[0], mask, kernel_back),
+        (nbr, grad_out[0], mask, weight_two),
     )
     grads = shape(weight_one.shape, F32)
     chunk = -(-32 * weight_one.shape[0] // (2 * owners * 16)) * 16
@@ -534,11 +547,12 @@
             pltpu.VMEM((BE, rows, width), F32),
             pltpu.VMEM((bricks,) + brick, F32),
             pltpu.VMEM((bricks,) + brick, BF16),
+            pltpu.VMEM((2, 9, 256, 128), BF16),
             pltpu.SemaphoreType.DMA((3, 2, send.shape[0])),
         ]
         + total
         + total,
-        (send, nbr, features[0], grad_out[0], mask, kernel_one, kernel_two, own_back, terms),
+        (send, nbr, features[0], grad_out[0], mask, weight_one, weight_two, own_back, terms),
         collective_id=0,
         has_side_effects=True,
     )

time: 70.2 us -> 68.6 us (0.977)
  other arithmetic: 1.67 us -> 0 us
  Pallas kernels: 61.8 us -> 62.6 us
    rev x1 -> x0, local copies, waits for them, and re-layouts: 1.04 us -> none  [per_device(): kernel_back = banded(jnp.flip(weight_two, 0).transpose(0, 2, 1))]
    unnamed x13 -> x15, local copies, waits for them, and re-layouts: 3.22 us -> 4.22 us
    concatenate x3 -> x0, other arithmetic: 0.97 us -> none  [banded(): return jnp.concatenate([left, right], axis=-1).reshape(9, 256, 128)]
    pallas_call x2, Pallas kernels: 61.8 us -> 62.6 us  [call(): pl.pallas_call(body, out_shape=outs, in_specs=specs, out_specs=[VM] * len...]
where the time goes in v3:
time: 68.6 us; the launch traced here: 68.4 us
  Pallas kernels  62.6 us (91%)
  local copies, waits for them, and re-layouts  5.13 us (7%)
  between operations  0.7 us (1%)
    pallas_call x2, Pallas kernels, call(): pl.pallas_call(body, out_shape=outs, in_specs=specs, out_specs=[VM] * len...  62.6 us
    unnamed x15, local copies, waits for them, and re-layouts  4.22 us

profile of v3, /device:TPU:1, one launch (start us, length us, event | category | flops | bytes accessed | tf_op | source)
XLA Modules:
  0.0 68.4 jit_solution(14581700497526752153)
XLA Ops:
  0.6 0.0 copy-start.5
  0.6 0.0 copy-start.1
  0.7 0.8 %copy.11.send_ref = s32[8,2]{1,0:T(8,128)S(1)} copy(s32[8,2]{0,1:T(2,128)} %bitcast.16) | data formatting | bytes 128 | tf_op jit(solution)/shard_map/squeeze | solution.py:494
  1.4 0.0 copy-done.5
  1.5 0.1 reshape_squeeze.3
  1.6 0.0 copy-start.4
  1.6 0.0 copy-done.1
  1.6 0.6 copy-done.4
  2.3 0.0 copy-start
  2.3 1.0 %copy-done = bf16[27,64,64]{2,1,0:T(8,128)(2,1)S(1)} copy-done((bf16[27,64,64]{2,1,0:T(8,128)(2,1)S(1)}, bf16[27,64,64]{2,1,0:T(8,128)(2,1)}, u32[]{:S(2)}) %copy-start) | copy-done | bytes 221208
  3.3 0.0 copy-start.2
  3.3 0.0 copy-start.3
  3.3 8.5 %shard_map.94 = (f32[4,8,8,512]{3,2,1,0:T(8,128)S(1)}, bf16[16,5,8,512]{3,2,1,0:T(8,128)(2,1)S(1)}) custom-call(s32[4,27]{1,0:T(4,128)S(1)} %bitcast.14, bf16[4,8,8,512]{3,2,1,0:T(8,128)(2,1)S(1)} %bitcast.10, s32[256,8]{1,0:T(8,128)S(1)} %bitcast.8, bf16[27,64,64]{2,1,0:T(8,128)(2,1)S(1)} %copy-done), custom_call_target="tpu_custom_call" | custom-call | tf_op jit(solution)/shard_map/pallas_call | solution.py:480
  11.8 0.0 copy-done.2
  11.8 0.0 copy-done.3
  11.8 54.1 %shard_map.95 = (bf16[4,8,8,512]{3,2,1,0:T(8,128)(2,1)S(1)}, f32[27,64,64]{2,1,0:T(8,128)S(1)}, f32[27,64,64]{2,1,0:T(8,128)S(1)}) custom-call(s32[8,2]{1,0:T(8,128)S(1)} %copy.11.send_ref, s32[4,27]{1,0:T(4,128)S(1)} %bitcast.15, bf16[4,8,8,512]{3,2,1,0:T(8,128)(2,1)S(1)} %bitcast.12, bf16[4,8,8,512]{3,2,1,0:T(8,128)(2,1)S(1)} %bitcast.11, ...), custom_call_target="tpu_custom_call" | custom-call | tf_op jit(solution)/shard_map/pallas_call | solution.py:480
  65.9 0.7 %copy.15 = bf16[1,4,8,8,512]{4,3,2,1,0:T(8,128)(2,1)} copy(bf16[1,4,8,8,512]{4,3,2,1,0:T(8,128)(2,1)S(1)} %bitcast.13) | data formatting | bytes 524288
  66.6 0.9 %copy.16 = f32[27,64,64]{2,1,0:T(8,128)} copy(f32[27,64,64]{2,1,0:T(8,128)S(1)} %get-tuple-element.17) | data formatting | bytes 884736
  67.5 0.9 %copy.17 = f32[27,64,64]{2,1,0:T(8,128)} copy(f32[27,64,64]{2,1,0:T(8,128)S(1)} %get-tuple-element.18) | data formatting | bytes 884736
  (1 shorter events, 0.0 us)
Async XLA Ops:
  0.6 0.8 %copy-start.5 = (s32[1,4,512]{2,1,0:T(4,128)S(1)}, s32[1,4,512]{2,1,0:T(4,128)}, u32[]{:S(2)}) copy-start(s32[1,4,512]{2,1,0:T(4,128)} %param.11) | copy-start | bytes 24580
  0.6 1.0 %copy-start.1 = (bf16[1,4,8,8,512]{4,3,2,1,0:T(8,128)(2,1)S(1)}, bf16[1,4,8,8,512]{4,3,2,1,0:T(8,128)(2,1)}, u32[]{:S(2)}) copy-start(bf16[1,4,8,8,512]{4,3,2,1,0:T(8,128)(2,1)} %param.10) | copy-start | bytes 786436
  1.6 0.7 %copy-start.4 = (s32[1,4,27]{2,1,0:T(4,128)S(1)}, s32[1,4,27]{2,1,0:T(4,128)}, u32[]{:S(2)}) copy-start(s32[1,4,27]{2,1,0:T(4,128)} %param.13) | copy-start | bytes 1300
  2.3 1.0 %copy-start = (bf16[27,64,64]{2,1,0:T(8,128)(2,1)S(1)}, bf16[27,64,64]{2,1,0:T(8,128)(2,1)}, u32[]{:S(2)}) copy-start(bf16[27,64,64]{2,1,0:T(8,128)(2,1)} %two_ref.1) | copy-start | bytes 663556
  3.3 8.5 %copy-start.2 = (bf16[27,64,64]{2,1,0:T(8,128)(2,1)S(1)}, bf16[27,64,64]{2,1,0:T(8,128)(2,1)}, u32[]{:S(2)}) copy-start(bf16[27,64,64]{2,1,0:T(8,128)(2,1)} %one_ref.1) | copy-start | bytes 663556
  3.3 8.5 %copy-start.3 = (bf16[1,4,8,8,512]{4,3,2,1,0:T(8,128)(2,1)S(1)}, bf16[1,4,8,8,512]{4,3,2,1,0:T(8,128)(2,1)}, u32[]{:S(2)}) copy-start(bf16[1,4,8,8,512]{4,3,2,1,0:T(8,128)(2,1)} %param.7) | copy-start | bytes 786436

commit v4 on v3

--- a/solution.py
+++ b/solution.py
@@ -410,13 +410,13 @@
     fill_outbound(send_ref, packed_ref, x_out, bricks)
     pl.semaphore_wait(barrier, owners)
     x_halo.start()
-    back_halo.start()
     for total in (one, two):
         size = 32 * grad_one_ref.shape[0]
         total.grad[size:, :] = jnp.zeros((total.grad.shape[0] - size, 128), F32)
     band_forward(one_ref, kernel_ref.at[0])
     band_forward(two_ref, kernel_ref.at[1])
     unpack_arrived(x_halo, slots, x_in, table_ref, bricks)
+    back_halo.start()
 
     assemble(table_ref, nbr_ref, shifted_ref)
     banded_conv(shifted_ref, kernel_ref.at[0], pre_ref)

time: 68.6 us -> 70.2 us (1.023)
  Pallas kernels: 62.6 us -> 64.1 us
    pallas_call x2, Pallas kernels: 62.6 us -> 64.1 us  [call(): pl.pallas_call(body, out_shape=outs, in_specs=specs, out_specs=[VM] * len...]
where the time goes in v4:
time: 70.2 us; the launch traced here: 69.9 us
  Pallas kernels  64.1 us (91%)
  local copies, waits for them, and re-layouts  5.13 us (7%)
    pallas_call x2, Pallas kernels, call(): pl.pallas_call(body, out_shape=outs, in_specs=specs, out_specs=[VM] * len...  64.1 us
    unnamed x15, local copies, waits for them, and re-layouts  4.22 us

profile of v4, /device:TPU:1, one launch (start us, length us, event | category | flops | bytes accessed | tf_op | source)
XLA Modules:
  0.0 69.9 jit_solution(2719073382785472996)
XLA Ops:
  0.6 0.0 copy-start.5
  0.6 0.0 copy-start.1
  0.7 0.8 %copy.11.send_ref = s32[8,2]{1,0:T(8,128)S(1)} copy(s32[8,2]{0,1:T(2,128)} %bitcast.16) | data formatting | bytes 128 | tf_op jit(solution)/shard_map/squeeze | solution.py:494
  1.4 0.0 copy-done.5
  1.5 0.1 reshape_squeeze.3
  1.6 0.0 copy-start.4
  1.6 0.0 copy-done.1
  1.6 0.6 copy-done.4
  2.3 0.0 copy-start
  2.3 1.0 %copy-done = bf16[27,64,64]{2,1,0:T(8,128)(2,1)S(1)} copy-done((bf16[27,64,64]{2,1,0:T(8,128)(2,1)S(1)}, bf16[27,64,64]{2,1,0:T(8,128)(2,1)}, u32[]{:S(2)}) %copy-start) | copy-done | bytes 221208
  3.3 0.0 copy-start.2
  3.3 0.0 copy-start.3
  3.3 8.5 %shard_map.94 = (f32[4,8,8,512]{3,2,1,0:T(8,128)S(1)}, bf16[16,5,8,512]{3,2,1,0:T(8,128)(2,1)S(1)}) custom-call(s32[4,27]{1,0:T(4,128)S(1)} %bitcast.14, bf16[4,8,8,512]{3,2,1,0:T(8,128)(2,1)S(1)} %bitcast.10, s32[256,8]{1,0:T(8,128)S(1)} %bitcast.8, bf16[27,64,64]{2,1,0:T(8,128)(2,1)S(1)} %copy-done), custom_call_target="tpu_custom_call" | custom-call | tf_op jit(solution)/shard_map/pallas_call | solution.py:480
  11.7 0.0 copy-done.2
  11.7 0.0 copy-done.3
  11.8 55.6 %shard_map.95 = (bf16[4,8,8,512]{3,2,1,0:T(8,128)(2,1)S(1)}, f32[27,64,64]{2,1,0:T(8,128)S(1)}, f32[27,64,64]{2,1,0:T(8,128)S(1)}) custom-call(s32[8,2]{1,0:T(8,128)S(1)} %copy.11.send_ref, s32[4,27]{1,0:T(4,128)S(1)} %bitcast.15, bf16[4,8,8,512]{3,2,1,0:T(8,128)(2,1)S(1)} %bitcast.12, bf16[4,8,8,512]{3,2,1,0:T(8,128)(2,1)S(1)} %bitcast.11, ...), custom_call_target="tpu_custom_call" | custom-call | tf_op jit(solution)/shard_map/pallas_call | solution.py:480
  67.4 0.7 %copy.15 = bf16[1,4,8,8,512]{4,3,2,1,0:T(8,128)(2,1)} copy(bf16[1,4,8,8,512]{4,3,2,1,0:T(8,128)(2,1)S(1)} %bitcast.13) | data formatting | bytes 524288
  68.1 0.9 %copy.16 = f32[27,64,64]{2,1,0:T(8,128)} copy(f32[27,64,64]{2,1,0:T(8,128)S(1)} %get-tuple-element.17) | data formatting | bytes 884736
  69.0 0.9 %copy.17 = f32[27,64,64]{2,1,0:T(8,128)} copy(f32[27,64,64]{2,1,0:T(8,128)S(1)} %get-tuple-element.18) | data formatting | bytes 884736
  (1 shorter events, 0.0 us)
Async XLA Ops:
  0.6 0.8 %copy-start.5 = (s32[1,4,512]{2,1,0:T(4,128)S(1)}, s32[1,4,512]{2,1,0:T(4,128)}, u32[]{:S(2)}) copy-start(s32[1,4,512]{2,1,0:T(4,128)} %param.11) | copy-start | bytes 24580
  0.6 1.0 %copy-start.1 = (bf16[1,4,8,8,512]{4,3,2,1,0:T(8,128)(2,1)S(1)}, bf16[1,4,8,8,512]{4,3,2,1,0:T(8,128)(2,1)}, u32[]{:S(2)}) copy-start(bf16[1,4,8,8,512]{4,3,2,1,0:T(8,128)(2,1)} %param.10) | copy-start | bytes 786436
  1.6 0.7 copy-start.4
  2.3 1.0 %copy-start = (bf16[27,64,64]{2,1,0:T(8,128)(2,1)S(1)}, bf16[27,64,64]{2,1,0:T(8,128)(2,1)}, u32[]{:S(2)}) copy-start(bf16[27,64,64]{2,1,0:T(8,128)(2,1)} %two_ref.1) | copy-start | bytes 663556
  3.3 8.5 %copy-start.2 = (bf16[27,64,64]{2,1,0:T(8,128)(2,1)S(1)}, bf16[27,64,64]{2,1,0:T(8,128)(2,1)}, u32[]{:S(2)}) copy-start(bf16[27,64,64]{2,1,0:T(8,128)(2,1)} %one_ref.1) | copy-start | bytes 663556
  3.3 8.5 %copy-start.3 = (bf16[1,4,8,8,512]{4,3,2,1,0:T(8,128)(2,1)S(1)}, bf16[1,4,8,8,512]{4,3,2,1,0:T(8,128)(2,1)}, u32[]{:S(2)}) copy-start(bf16[1,4,8,8,512]{4,3,2,1,0:T(8,128)(2,1)} %param.7) | copy-start | bytes 786436
